TPU v7x, 32 devices: a whole 2x2x4 slice. The times are simulated.
32 devices in a mesh: dp: 1, expert: 32 (over z, y, x, core).
Axes of the slice: x: 2, y: 2, z: 4, core: 2. Of those that a mesh axis runs over, the one named last changes fastest.
Arguments:
- tokens: bfloat16 [4096, 3584], P('expert', 'dp'), may hold values from -6 to 6
- cotangent: bfloat16 [4096, 3584], P('expert', 'dp'), may hold values from -6 to 6
- expert_ids: int32 [4096, 4], P('expert'), may hold values from 0 to 27, all different within a row; in each aligned block of 128 rows (0 to 127, 128 to 255, ...) at most 22 rows name the same one
- gate_probs: bfloat16 [4096, 4], P('expert'), may hold values from 0.049804688 to 1
- slot_expert: int32 [32], replicated, may hold values from 0 to 27, as said below
- w_gate: bfloat16 [32, 3584, 1024], P('expert', None, 'dp'), as said below
- w_up: bfloat16 [32, 3584, 1024], P('expert', None, 'dp'), as said below
- w_down: bfloat16 [32, 1024, 3584], P('expert', 'dp'), as said below
Outputs:
- d_tokens: bfloat16 [4096, 3584], P('expert', 'dp')
- d_probs: float32 [4096, 4], P('expert')
- grad_gate: bfloat16 [32, 3584, 1024], P('expert', None, 'dp')
- grad_up: bfloat16 [32, 3584, 1024], P('expert', None, 'dp')
- grad_down: bfloat16 [32, 1024, 3584], P('expert', 'dp')
Inputs may be any that keep to these rules, and one draw needn't show every extreme that they name: `expert_ids`: in each aligned block of 128 rows no expert is named by more than 22 rows, a bound that some block reaches. `slot_expert`: every expert appears once or twice; an expert that appears twice holds slots 2 j and 2 j + 1 for some j, and 4 experts appear twice. `w_gate`: slots that hold the same expert hold equal weights. `w_up`: slots that hold the same expert hold equal weights. `w_down`: slots that hold the same expert hold equal weights.
All inputs are finite; a program needn't handle non-finite values.
Results may differ from a plain program's by a relative error of at most 0.015.
Values may be sent and summed in bfloat16 or wider, within the bound.
A program may use at most 256 MiB of HBM per device.

v0:
```python
import jax
import jax.numpy as jnp
from jax import lax
from jax.sharding import PartitionSpec as P


def partner_2(x, axis, apart):
    return lax.ppermute(x, axis, [(i, i ^ 1 << apart) for i in range(lax.axis_size(axis))])


def silu_parts(gate):
    sig = jax.nn.sigmoid(gate)
    return (gate * sig, sig * (1.0 + gate * (1.0 - sig)))


def contract(left, right, left_dim, right_dim):
    return lax.dot_general(
        left, right, (((left_dim,), (right_dim,)), ((), ())), preferred_element_type=jnp.float32
    )


def shards(tokens, cotangent, expert_ids, gate_probs, slot_expert, w_gate, w_up, w_down):
    slots = lax.axis_size("expert")
    here = lax.axis_index("expert")
    tok_rows, quarter = tokens.shape
    top = expert_ids.shape[1]
    experts = slots - max(2, slots // 8)
    capacity = max(2, 5 * tok_rows * top // (4 * experts))
    width = w_gate.shape[1]
    assigns = tok_rows * top
    tile = 128
    flat_ids = expert_ids.reshape(assigns)
    flat_probs = gate_probs.reshape(assigns)
    expert_range = jnp.arange(experts, dtype=jnp.int32)
    holds = (slot_expert[None, :] == expert_range[:, None]).astype(jnp.int32)
    first_slot = jnp.argmax(holds, axis=1)
    last_slot = slots - 1 - jnp.argmax(holds[:, ::-1], axis=1)
    picks = (flat_ids[:, None] == expert_range[None, :]).astype(jnp.int32)
    before = jnp.cumsum(picks, axis=0) - picks
    rank = jnp.sum(before * picks, axis=1)
    slot_one = jnp.sum(picks * first_slot[None, :], axis=1)
    slot_two = jnp.sum(picks * last_slot[None, :], axis=1)
    paired = slot_one != slot_two
    shifted = rank + here % 2
    target = jnp.where(paired & (shifted % 2 == 1), slot_two, slot_one)
    place = jnp.where(paired, shifted // 2, rank)
    flat_pos = target * capacity + place
    total = slots * capacity
    source_row = (
        jnp.full((total,), tok_rows, jnp.int32)
        .at[flat_pos]
        .set(jnp.arange(assigns, dtype=jnp.int32) // top)
    )
    send_probs = (
        jnp.zeros((total,), jnp.bfloat16).at[flat_pos].set(flat_probs).reshape(slots, capacity)
    )

    def pack(rows):
        padded = jnp.concatenate([rows, jnp.zeros((1, rows.shape[1]), rows.dtype)], axis=0)
        return padded[source_row].reshape(slots, capacity, rows.shape[1])

    part_x, part_dy, recv_p = (
        lax.all_to_all(pack(tokens), "expert", split_axis=0, concat_axis=0, tiled=True),
        lax.all_to_all(pack(cotangent), "expert", split_axis=0, concat_axis=0, tiled=True),
        lax.all_to_all(send_probs, "expert", split_axis=0, concat_axis=0, tiled=True),
    )
    recv_x, recv_dy = (
        lax.all_gather(part_x, "dp", axis=2, tiled=True),
        lax.all_gather(part_dy, "dp", axis=2, tiled=True),
    )
    padded_total = (total + tile - 1) // tile * tile
    rows_x = recv_x.reshape(total, width)
    rows_dy = recv_dy.reshape(total, width)
    rows_p = recv_p.reshape(total)
    wg = w_gate[0]
    wu = w_up[0]
    wd = w_down[0]
    share = wg.shape[1]
    extra = padded_total - total
    work_x = jnp.concatenate([rows_x, jnp.zeros((extra, width), rows_x.dtype)], axis=0)
    work_dy = jnp.concatenate([rows_dy, jnp.zeros((extra, width), rows_dy.dtype)], axis=0)
    work_p = jnp.concatenate([rows_p, jnp.zeros((extra,), rows_p.dtype)], axis=0)
    tiles = padded_total // tile

    def tile_step(index, carry):
        acc_gate, acc_up, acc_down, pieces, scores = carry
        start = index * tile
        xs = lax.dynamic_slice_in_dim(work_x, start, tile, 0)
        dys = lax.dynamic_slice_in_dim(work_dy, start, tile, 0)
        probs = lax.dynamic_slice_in_dim(work_p, start, tile, 0)
        gate = jnp.dot(xs, wg, preferred_element_type=jnp.float32)
        up = jnp.dot(xs, wu, preferred_element_type=jnp.float32)
        act, slope = silu_parts(gate)
        hidden = (act * up).astype(jnp.bfloat16)
        out = jnp.dot(hidden, wd, preferred_element_type=jnp.float32)
        score = jnp.sum(dys.astype(jnp.float32) * out, axis=1)
        d_out = (probs.astype(jnp.float32)[:, None] * dys.astype(jnp.float32)).astype(jnp.bfloat16)
        d_hidden = contract(d_out, wd, 1, 1)
        d_gate_pre = (d_hidden * up * slope).astype(jnp.bfloat16)
        d_up_pre = (d_hidden * act).astype(jnp.bfloat16)
        acc_down = acc_down + contract(hidden, d_out, 0, 0)
        acc_gate = acc_gate + contract(xs, d_gate_pre, 0, 0)
        acc_up = acc_up + contract(xs, d_up_pre, 0, 0)
        piece = contract(d_gate_pre, wg, 1, 1) + contract(d_up_pre, wu, 1, 1)
        pieces = lax.dynamic_update_slice_in_dim(pieces, piece.astype(jnp.bfloat16), start, 0)
        scores = lax.dynamic_update_slice_in_dim(scores, score, start, 0)
        return (acc_gate, acc_up, acc_down, pieces, scores)

    init = (
        jnp.zeros((width, share), jnp.float32),
        jnp.zeros((width, share), jnp.float32),
        jnp.zeros((share, width), jnp.float32),
        jnp.zeros((padded_total, width), jnp.bfloat16),
        jnp.zeros((padded_total,), jnp.float32),
    )
    acc_gate, acc_up, acc_down, pieces, scores = lax.fori_loop(0, tiles, tile_step, init)
    row_pieces = pieces[:total]
    row_scores = scores[:total]
    summed = lax.psum_scatter(
        row_pieces.reshape(slots, capacity, width), "dp", scatter_dimension=2, tiled=True
    ).astype(jnp.float32)
    total_scores = lax.psum(row_scores.reshape(slots, capacity), "dp")
    back_x, back_s = (
        lax.all_to_all(
            summed.astype(jnp.bfloat16), "expert", split_axis=0, concat_axis=0, tiled=True
        ).astype(summed.dtype),
        lax.all_to_all(
            total_scores.astype(jnp.bfloat16), "expert", split_axis=0, concat_axis=0, tiled=True
        ).astype(total_scores.dtype),
    )
    per_assign = back_x.reshape(total, quarter)[flat_pos].reshape(tok_rows, top, quarter)
    d_tokens = jnp.sum(per_assign, axis=1).astype(jnp.bfloat16)
    d_probs = back_s.reshape(total)[flat_pos].reshape(tok_rows, top)
    partner = jnp.bitwise_xor(here, 1)
    same = slot_expert[here] == slot_expert[partner]
    got_gate, got_up, got_down = (
        partner_2(acc_gate.astype(jnp.bfloat16), "expert", 0).astype(acc_gate.dtype),
        partner_2(acc_up.astype(jnp.bfloat16), "expert", 0).astype(acc_up.dtype),
        partner_2(acc_down.astype(jnp.bfloat16), "expert", 0).astype(acc_down.dtype),
    )
    grad_gate = (acc_gate + jnp.where(same, got_gate, 0.0)).astype(jnp.bfloat16)[None]
    grad_up = (acc_up + jnp.where(same, got_up, 0.0)).astype(jnp.bfloat16)[None]
    grad_down = (acc_down + jnp.where(same, got_down, 0.0)).astype(jnp.bfloat16)[None]
    return (d_tokens, d_probs, grad_gate, grad_up, grad_down)


def solution(mesh):
    placed = (
        P("expert", "dp"),
        P("expert", "dp"),
        P("expert", None),
        P("expert", None),
        P(),
        P("expert", None, "dp"),
        P("expert", None, "dp"),
        P("expert", "dp", None),
    )
    return jax.shard_map(
        shards,
        mesh=mesh,
        in_specs=placed,
        out_specs=(
            P("expert", "dp"),
            P("expert", None),
            P("expert", None, "dp"),
            P("expert", None, "dp"),
            P("expert", "dp", None),
        ),
        check_vma=False,
    )
```

profile of v0, /device:TPU:0, one launch (start us, length us, event | category | flops | bytes accessed | tf_op | source)
XLA Modules:
  0.0 870.7 jit_solution(9395069342687048809)
XLA Ops:
  11.5 7.3 all-to-all-start.1
  27.8 7.5 reshape.198
  35.3 5.9 all-to-all-start
  46.6 7.5 reshape.202
  54.1 109.7 %all-to-all-done = bf16[32,22,3584]{2,1,0:T(8,128)(2,1)} async-done(((bf16[32,22,3584]{2,1,0:T(8,128)(2,1)}), bf16[32,22,3584]{2,1,0:T(8,128)(2,1)}, u32[]{:S(2)}, u32[]{:S(2)}) %all-to-all-start) | async-done | bytes 5046304 | tf_op jit(solution)/shard_map/all_to_all | solution.py:63
  167.6 7.6 reshape.199
  175.2 5.2 concatenate.16
  180.5 109.5 %all-to-all-done.2 = bf16[32,22,3584]{2,1,0:T(8,128)(2,1)} async-done(((bf16[32,22,3584]{2,1,0:T(8,128)(2,1)}), bf16[32,22,3584]{2,1,0:T(8,128)(2,1)}, u32[]{:S(2)}, u32[]{:S(2)}) %all-to-all-start.2) | async-done | bytes 5046304 | tf_op jit(solution)/shard_map/all_to_all | solution.py:64
  289.9 7.6 reshape.203
  297.5 5.2 concatenate.19
  305.6 363.3 %while.22 = (s32[]{:T(128)}, f32[3584,1024]{1,0:T(8,128)}, f32[3584,1024]{1,0:T(8,128)}, f32[1024,3584]{1,0:T(8,128)}, bf16[768,3584]{1,0:T(8,128)(2,1)}, /*inde...) while((s32[]{:T(128)}, f32[3584,1024]{1,0:T(8,128)}, ...), condition=%wide.region_11.12_spmd.clone, body=%wide.region_9.11_spmd.clone.sunk | while | flops 8484749312 | bytes 347868224 | solution.py:116
  305.9 6.0 fusion.88
  317.1 8.7 select_add_fusion.8
  325.7 10.9 %select_add_fusion.7 = f32[3584,1024]{1,0:T(8,128)} fusion(f32[3584,1024]{1,0:T(8,128)} %get-tuple-element.400, bf16[128,1024]{1,0:T(8,128)(2,1)S(1)} %get-tuple-element.380, pred[]{:T(512)S(6)} %compare.24, bf16[768,3584]{1,0:T(8,128)(2,1)} %get-tuple-element.420, s32[]{:T(128)S(6)} %select_n.159), kind=kOutput, calls=%fused_computation.7.clone.1 | convolution fusion | flops 946864128 | bytes 30539780 | tf_op jit(solution)/shard_map/while/body/eval_jaxpr/dot_general | solution.py:17
  344.4 10.3 %fusion.90 = bf16[768,3584]{1,0:T(8,128)(2,1)} fusion(bf16[768,3584]{1,0:T(8,128)(2,1)} %get-tuple-element.402, s32[]{:T(128)S(6)} %select_n.159, f32[128,3584]{1,0:T(8,128)S(1)} %fusion.89, bf16[128,1024]{1,0:T(8,128)(2,1)S(1)} %copy-done.3, bf16[3584,1024]{1,0:T(8,128)(2,1)} %get-tuple-element.424), kind=kOutput, calls=%fused_computation.12.clone.1 | convolution fusion | flops 940441600 | bytes 10354692 | tf_op jit(solution)/shard_map/while/body/eval_jaxpr/dot_general | solution.py:17
  357.5 6.0 fusion.88
  368.7 12.9 %select_add_fusion.8 = f32[1024,3584]{1,0:T(8,128)} fusion(f32[1024,3584]{1,0:T(8,128)} %get-tuple-element.401, bf16[128,1024]{1,0:T(8,128)(2,1)S(1)} %get-tuple-element.381, pred[]{:T(512)S(6)} %compare.24, f32[128]{0:T(128)S(1)} %dynamic-slice_convert_fusion.2, bf16[768,3584]{1,0:T(8,128)(2,1)} %get-tuple-element.422, s32[]{:T(128)S(6)} %select_n.159), kind=kOutput, calls=%fused_computation.6.clone.1 | convolution fusion | flops 948240384 | bytes 30540292 | tf_op jit(solution)/shard_map/while/body/eval_jaxpr/dot_general | solution.py:17
  381.6 15.1 %select_add_fusion.7 = f32[3584,1024]{1,0:T(8,128)} fusion(f32[3584,1024]{1,0:T(8,128)} %get-tuple-element.400, bf16[128,1024]{1,0:T(8,128)(2,1)S(1)} %get-tuple-element.380, pred[]{:T(512)S(6)} %compare.24, bf16[768,3584]{1,0:T(8,128)(2,1)} %get-tuple-element.420, s32[]{:T(128)S(6)} %select_n.159), kind=kOutput, calls=%fused_computation.7.clone.1 | convolution fusion | flops 946864128 | bytes 30539780 | tf_op jit(solution)/shard_map/while/body/eval_jaxpr/dot_general | solution.py:17
  404.6 10.3 %fusion.90 = bf16[768,3584]{1,0:T(8,128)(2,1)} fusion(bf16[768,3584]{1,0:T(8,128)(2,1)} %get-tuple-element.402, s32[]{:T(128)S(6)} %select_n.159, f32[128,3584]{1,0:T(8,128)S(1)} %fusion.89, bf16[128,1024]{1,0:T(8,128)(2,1)S(1)} %copy-done.3, bf16[3584,1024]{1,0:T(8,128)(2,1)} %get-tuple-element.424), kind=kOutput, calls=%fused_computation.12.clone.1 | convolution fusion | flops 940441600 | bytes 10354692 | tf_op jit(solution)/shard_map/while/body/eval_jaxpr/dot_general | solution.py:17
  417.7 6.0 fusion.88
  428.8 12.9 %select_add_fusion.8 = f32[1024,3584]{1,0:T(8,128)} fusion(f32[1024,3584]{1,0:T(8,128)} %get-tuple-element.401, bf16[128,1024]{1,0:T(8,128)(2,1)S(1)} %get-tuple-element.381, pred[]{:T(512)S(6)} %compare.24, f32[128]{0:T(128)S(1)} %dynamic-slice_convert_fusion.2, bf16[768,3584]{1,0:T(8,128)(2,1)} %get-tuple-element.422, s32[]{:T(128)S(6)} %select_n.159), kind=kOutput, calls=%fused_computation.6.clone.1 | convolution fusion | flops 948240384 | bytes 30540292 | tf_op jit(solution)/shard_map/while/body/eval_jaxpr/dot_general | solution.py:17
  441.8 15.1 %select_add_fusion.7 = f32[3584,1024]{1,0:T(8,128)} fusion(f32[3584,1024]{1,0:T(8,128)} %get-tuple-element.400, bf16[128,1024]{1,0:T(8,128)(2,1)S(1)} %get-tuple-element.380, pred[]{:T(512)S(6)} %compare.24, bf16[768,3584]{1,0:T(8,128)(2,1)} %get-tuple-element.420, s32[]{:T(128)S(6)} %select_n.159), kind=kOutput, calls=%fused_computation.7.clone.1 | convolution fusion | flops 946864128 | bytes 30539780 | tf_op jit(solution)/shard_map/while/body/eval_jaxpr/dot_general | solution.py:17
  464.8 10.3 %fusion.90 = bf16[768,3584]{1,0:T(8,128)(2,1)} fusion(bf16[768,3584]{1,0:T(8,128)(2,1)} %get-tuple-element.402, s32[]{:T(128)S(6)} %select_n.159, f32[128,3584]{1,0:T(8,128)S(1)} %fusion.89, bf16[128,1024]{1,0:T(8,128)(2,1)S(1)} %copy-done.3, bf16[3584,1024]{1,0:T(8,128)(2,1)} %get-tuple-element.424), kind=kOutput, calls=%fused_computation.12.clone.1 | convolution fusion | flops 940441600 | bytes 10354692 | tf_op jit(solution)/shard_map/while/body/eval_jaxpr/dot_general | solution.py:17
  477.9 6.0 fusion.88
  489.0 12.9 %select_add_fusion.8 = f32[1024,3584]{1,0:T(8,128)} fusion(f32[1024,3584]{1,0:T(8,128)} %get-tuple-element.401, bf16[128,1024]{1,0:T(8,128)(2,1)S(1)} %get-tuple-element.381, pred[]{:T(512)S(6)} %compare.24, f32[128]{0:T(128)S(1)} %dynamic-slice_convert_fusion.2, bf16[768,3584]{1,0:T(8,128)(2,1)} %get-tuple-element.422, s32[]{:T(128)S(6)} %select_n.159), kind=kOutput, calls=%fused_computation.6.clone.1 | convolution fusion | flops 948240384 | bytes 30540292 | tf_op jit(solution)/shard_map/while/body/eval_jaxpr/dot_general | solution.py:17
  502.0 15.1 %select_add_fusion.7 = f32[3584,1024]{1,0:T(8,128)} fusion(f32[3584,1024]{1,0:T(8,128)} %get-tuple-element.400, bf16[128,1024]{1,0:T(8,128)(2,1)S(1)} %get-tuple-element.380, pred[]{:T(512)S(6)} %compare.24, bf16[768,3584]{1,0:T(8,128)(2,1)} %get-tuple-element.420, s32[]{:T(128)S(6)} %select_n.159), kind=kOutput, calls=%fused_computation.7.clone.1 | convolution fusion | flops 946864128 | bytes 30539780 | tf_op jit(solution)/shard_map/while/body/eval_jaxpr/dot_general | solution.py:17
  524.9 10.3 %fusion.90 = bf16[768,3584]{1,0:T(8,128)(2,1)} fusion(bf16[768,3584]{1,0:T(8,128)(2,1)} %get-tuple-element.402, s32[]{:T(128)S(6)} %select_n.159, f32[128,3584]{1,0:T(8,128)S(1)} %fusion.89, bf16[128,1024]{1,0:T(8,128)(2,1)S(1)} %copy-done.3, bf16[3584,1024]{1,0:T(8,128)(2,1)} %get-tuple-element.424), kind=kOutput, calls=%fused_computation.12.clone.1 | convolution fusion | flops 940441600 | bytes 10354692 | tf_op jit(solution)/shard_map/while/body/eval_jaxpr/dot_general | solution.py:17
  538.0 6.0 fusion.88
  549.2 12.9 %select_add_fusion.8 = f32[1024,3584]{1,0:T(8,128)} fusion(f32[1024,3584]{1,0:T(8,128)} %get-tuple-element.401, bf16[128,1024]{1,0:T(8,128)(2,1)S(1)} %get-tuple-element.381, pred[]{:T(512)S(6)} %compare.24, f32[128]{0:T(128)S(1)} %dynamic-slice_convert_fusion.2, bf16[768,3584]{1,0:T(8,128)(2,1)} %get-tuple-element.422, s32[]{:T(128)S(6)} %select_n.159), kind=kOutput, calls=%fused_computation.6.clone.1 | convolution fusion | flops 948240384 | bytes 30540292 | tf_op jit(solution)/shard_map/while/body/eval_jaxpr/dot_general | solution.py:17
  562.1 15.1 %select_add_fusion.7 = f32[3584,1024]{1,0:T(8,128)} fusion(f32[3584,1024]{1,0:T(8,128)} %get-tuple-element.400, bf16[128,1024]{1,0:T(8,128)(2,1)S(1)} %get-tuple-element.380, pred[]{:T(512)S(6)} %compare.24, bf16[768,3584]{1,0:T(8,128)(2,1)} %get-tuple-element.420, s32[]{:T(128)S(6)} %select_n.159), kind=kOutput, calls=%fused_computation.7.clone.1 | convolution fusion | flops 946864128 | bytes 30539780 | tf_op jit(solution)/shard_map/while/body/eval_jaxpr/dot_general | solution.py:17
  585.1 10.3 %fusion.90 = bf16[768,3584]{1,0:T(8,128)(2,1)} fusion(bf16[768,3584]{1,0:T(8,128)(2,1)} %get-tuple-element.402, s32[]{:T(128)S(6)} %select_n.159, f32[128,3584]{1,0:T(8,128)S(1)} %fusion.89, bf16[128,1024]{1,0:T(8,128)(2,1)S(1)} %copy-done.3, bf16[3584,1024]{1,0:T(8,128)(2,1)} %get-tuple-element.424), kind=kOutput, calls=%fused_computation.12.clone.1 | convolution fusion | flops 940441600 | bytes 10354692 | tf_op jit(solution)/shard_map/while/body/eval_jaxpr/dot_general | solution.py:17
  598.2 6.0 fusion.88
  609.3 12.9 %select_add_fusion.8 = f32[1024,3584]{1,0:T(8,128)} fusion(f32[1024,3584]{1,0:T(8,128)} %get-tuple-element.401, bf16[128,1024]{1,0:T(8,128)(2,1)S(1)} %get-tuple-element.381, pred[]{:T(512)S(6)} %compare.24, f32[128]{0:T(128)S(1)} %dynamic-slice_convert_fusion.2, bf16[768,3584]{1,0:T(8,128)(2,1)} %get-tuple-element.422, s32[]{:T(128)S(6)} %select_n.159), kind=kOutput, calls=%fused_computation.6.clone.1 | convolution fusion | flops 948240384 | bytes 30540292 | tf_op jit(solution)/shard_map/while/body/eval_jaxpr/dot_general | solution.py:17
  622.3 15.1 %select_add_fusion.7 = f32[3584,1024]{1,0:T(8,128)} fusion(f32[3584,1024]{1,0:T(8,128)} %get-tuple-element.400, bf16[128,1024]{1,0:T(8,128)(2,1)S(1)} %get-tuple-element.380, pred[]{:T(512)S(6)} %compare.24, bf16[768,3584]{1,0:T(8,128)(2,1)} %get-tuple-element.420, s32[]{:T(128)S(6)} %select_n.159), kind=kOutput, calls=%fused_computation.7.clone.1 | convolution fusion | flops 946864128 | bytes 30539780 | tf_op jit(solution)/shard_map/while/body/eval_jaxpr/dot_general | solution.py:17
  645.2 10.3 %fusion.90 = bf16[768,3584]{1,0:T(8,128)(2,1)} fusion(bf16[768,3584]{1,0:T(8,128)(2,1)} %get-tuple-element.402, s32[]{:T(128)S(6)} %select_n.159, f32[128,3584]{1,0:T(8,128)S(1)} %fusion.89, bf16[128,1024]{1,0:T(8,128)(2,1)S(1)} %copy-done.3, bf16[3584,1024]{1,0:T(8,128)(2,1)} %get-tuple-element.424), kind=kOutput, calls=%fused_computation.12.clone.1 | convolution fusion | flops 940441600 | bytes 10354692 | tf_op jit(solution)/shard_map/while/body/eval_jaxpr/dot_general | solution.py:17
  668.9 9.1 %convert_element_type.124 = bf16[1024,3584]{1,0:T(8,128)(2,1)} convert(f32[1024,3584]{1,0:T(8,128)} %get-tuple-element.216) | non-fusion elementwise | flops 3670016 | bytes 22020096 | tf_op jit(solution)/shard_map/convert_element_type | solution.py:139
  678.0 9.4 %convert_element_type.121 = bf16[3584,1024]{1,0:T(8,128)(2,1)} convert(f32[3584,1024]{1,0:T(8,128)} %get-tuple-element.215) | non-fusion elementwise | flops 3670016 | bytes 22020096 | tf_op jit(solution)/shard_map/convert_element_type | solution.py:138
  697.0 7.5 reshape.204
  704.5 5.9 all-to-all-start.3
  710.5 9.4 %convert_element_type.118 = bf16[3584,1024]{1,0:T(8,128)(2,1)} convert(f32[3584,1024]{1,0:T(8,128)} %get-tuple-element.214) | non-fusion elementwise | flops 3670016 | bytes 22020096 | tf_op jit(solution)/shard_map/convert_element_type | solution.py:137
  725.1 11.1 %fusion.22 = bf16[1,1024,3584]{2,1,0:T(8,128)(2,1)} fusion(f32[1024,3584]{1,0:T(8,128)} %get-tuple-element.216, bf16[1024,3584]{1,0:T(8,128)(2,1)} %collective-permute-done.2, pred[]{:T(512)} %bitcast.8), kind=kLoop, calls=%fused_computation.40 | loop fusion | flops 14680064 | bytes 29360128 | tf_op jit(solution)/shard_map/broadcast_in_dim | solution.py:143
  736.2 11.7 %fusion.21 = bf16[1,3584,1024]{2,1,0:T(8,128)(2,1)} fusion(f32[3584,1024]{1,0:T(8,128)} %get-tuple-element.215, bf16[3584,1024]{1,0:T(8,128)(2,1)} %collective-permute-done.1, pred[]{:T(512)} %bitcast.8), kind=kLoop, calls=%fused_computation.39 | loop fusion | flops 14680064 | bytes 29360128 | tf_op jit(solution)/shard_map/broadcast_in_dim | solution.py:142
  748.0 7.6 fusion.20
  755.6 77.4 %all-to-all-done.3 = bf16[32,22,3584]{2,1,0:T(8,128)(2,1)} async-done(((bf16[32,22,3584]{2,1,0:T(8,128)(2,1)}), bf16[32,22,3584]{2,1,0:T(8,128)(2,1)}, u32[]{:S(2)}, u32[]{:S(2)}) %all-to-all-start.3) | async-done | bytes 5046304 | tf_op jit(solution)/shard_map/all_to_all | solution.py:124
  833.0 8.3 reshape.210
  841.3 12.0 %gather_fusion.2 = f32[512,3584]{1,0:T(8,128)} fusion(f32[704,3584]{1,0:T(8,128)} %reshape.210, s32[1024]{0:T(1024)S(1)} %pad_clamp_fusion), kind=kCustom, calls=%fused_computation.2 | custom fusion | bytes 14682112 | tf_op jit(solution)/shard_map/gather | solution.py:131
  853.3 8.8 %reshape.207 = f32[128,4,3584]{2,1,0:T(4,128)} reshape(f32[512,3584]{1,0:T(8,128)} %gather_fusion.2) | data formatting | bytes 14680064 | tf_op jit(solution)/shard_map/reshape | solution.py:131
  862.1 8.5 reduce_sum.61
  (309 shorter events, 138.2 us)
Async XLA Ops:
  11.5 23.8 %all-to-all-start.1 = ((bf16[32,1,22]{2,1,0:T(2,128)(2,1)}), bf16[32,1,22]{2,1,0:T(2,128)(2,1)S(1)}, u32[]{:S(2)}, u32[]{:S(2)}) async-start(bf16[32,1,22]{2,1,0:T(2,128)(2,1)} %all_to_all.25), calls=%async_computation.1 | async-start | bytes 32768 | tf_op jit(solution)/shard_map/all_to_all | solution.py:65
  35.3 128.5 %all-to-all-start = ((bf16[32,22,3584]{2,1,0:T(8,128)(2,1)}), bf16[32,22,3584]{2,1,0:T(8,128)(2,1)}, u32[]{:S(2)}, u32[]{:S(2)}) async-start(bf16[32,22,3584]{2,1,0:T(8,128)(2,1)} %reshape.198), calls=%async_computation | async-start | bytes 11010048 | tf_op jit(solution)/shard_map/all_to_all | solution.py:63
  163.8 126.1 %all-to-all-start.2 = ((bf16[32,22,3584]{2,1,0:T(8,128)(2,1)}), bf16[32,22,3584]{2,1,0:T(8,128)(2,1)}, u32[]{:S(2)}, u32[]{:S(2)}) async-start(bf16[32,22,3584]{2,1,0:T(8,128)(2,1)} %reshape.202), calls=%async_computation.2 | async-start | bytes 11010048 | tf_op jit(solution)/shard_map/all_to_all | solution.py:64
  325.7 16.1 %slice-start.8 = ((s8[7340032]{0:T(1024)(128)(4,1)}), s8[4194304]{0:T(1024)(128)(4,1)S(1)}, s32[]{:S(2)}) async-start(s8[7340032]{0:T(1024)(128)(4,1)} %bitcast.65), calls=%async_computation.13 | async-start | bytes 8388608 | tf_op jit(solution)/shard_map/while
  341.9 12.9 %copy-start = (f32[3584,1024]{1,0:T(8,128)}, f32[3584,1024]{1,0:T(8,128)S(1)}, u32[]{:S(2)}) copy-start(f32[3584,1024]{1,0:T(8,128)S(1)} %select_add_fusion.6) | copy-start | bytes 44040196 | tf_op jit(solution)/shard_map/while
  368.7 13.0 %copy-start.2 = (bf16[128,1024]{1,0:T(8,128)(2,1)}, bf16[128,1024]{1,0:T(8,128)(2,1)S(1)}, u32[]{:S(2)}) copy-start(bf16[128,1024]{1,0:T(8,128)(2,1)S(1)} %get-tuple-element.380) | copy-start | bytes 786436 | tf_op jit(solution)/shard_map/while
  381.6 15.2 %slice-start = ((s8[14680064]{0:T(1024)(128)(4,1)}), s8[4194304]{0:T(1024)(128)(4,1)S(1)}, s32[]{:S(2)}) async-start(s8[14680064]{0:T(1024)(128)(4,1)} %bitcast.60), calls=%async_computation.5 | async-start | bytes 8388608 | tf_op jit(solution)/shard_map/while
  381.6 15.2 %slice-start.1 = ((s8[14680064]{0:T(1024)(128)(4,1)}), s8[4194304]{0:T(1024)(128)(4,1)S(1)}, s32[]{:S(2)}) async-start(s8[14680064]{0:T(1024)(128)(4,1)} %bitcast.60), calls=%async_computation.6 | async-start | bytes 8388608 | tf_op jit(solution)/shard_map/while
  381.6 15.2 %slice-start.2 = ((s8[14680064]{0:T(1024)(128)(4,1)}), s8[4194304]{0:T(1024)(128)(4,1)S(1)}, s32[]{:S(2)}) async-start(s8[14680064]{0:T(1024)(128)(4,1)} %bitcast.60), calls=%async_computation.7 | async-start | bytes 8388608 | tf_op jit(solution)/shard_map/while
  381.6 15.2 %slice-start.3 = ((s8[14680064]{0:T(1024)(128)(4,1)}), s8[2097152]{0:T(1024)(128)(4,1)S(1)}, s32[]{:S(2)}) async-start(s8[14680064]{0:T(1024)(128)(4,1)} %bitcast.60), calls=%async_computation.8 | async-start | bytes 4194304 | tf_op jit(solution)/shard_map/while
  381.6 20.4 %slice-start.8 = ((s8[7340032]{0:T(1024)(128)(4,1)}), s8[4194304]{0:T(1024)(128)(4,1)S(1)}, s32[]{:S(2)}) async-start(s8[7340032]{0:T(1024)(128)(4,1)} %bitcast.65), calls=%async_computation.13 | async-start | bytes 8388608 | tf_op jit(solution)/shard_map/while
  402.0 13.0 %copy-start = (f32[3584,1024]{1,0:T(8,128)}, f32[3584,1024]{1,0:T(8,128)S(1)}, u32[]{:S(2)}) copy-start(f32[3584,1024]{1,0:T(8,128)S(1)} %select_add_fusion.6) | copy-start | bytes 44040196 | tf_op jit(solution)/shard_map/while
  402.0 12.9 %slice-start.10 = ((s8[7340032]{0:T(1024)(128)(4,1)}), s8[3145728]{0:T(1024)(128)(4,1)S(1)}, s32[]{:S(2)}) async-start(s8[7340032]{0:T(1024)(128)(4,1)} %bitcast.68), calls=%async_computation.15 | async-start | bytes 6291456 | tf_op jit(solution)/shard_map/while
  428.8 13.0 %copy-start.2 = (bf16[128,1024]{1,0:T(8,128)(2,1)}, bf16[128,1024]{1,0:T(8,128)(2,1)S(1)}, u32[]{:S(2)}) copy-start(bf16[128,1024]{1,0:T(8,128)(2,1)S(1)} %get-tuple-element.380) | copy-start | bytes 786436 | tf_op jit(solution)/shard_map/while
  441.8 15.2 %slice-start = ((s8[14680064]{0:T(1024)(128)(4,1)}), s8[4194304]{0:T(1024)(128)(4,1)S(1)}, s32[]{:S(2)}) async-start(s8[14680064]{0:T(1024)(128)(4,1)} %bitcast.60), calls=%async_computation.5 | async-start | bytes 8388608 | tf_op jit(solution)/shard_map/while
  441.8 15.2 %slice-start.1 = ((s8[14680064]{0:T(1024)(128)(4,1)}), s8[4194304]{0:T(1024)(128)(4,1)S(1)}, s32[]{:S(2)}) async-start(s8[14680064]{0:T(1024)(128)(4,1)} %bitcast.60), calls=%async_computation.6 | async-start | bytes 8388608 | tf_op jit(solution)/shard_map/while
  441.8 15.2 %slice-start.2 = ((s8[14680064]{0:T(1024)(128)(4,1)}), s8[4194304]{0:T(1024)(128)(4,1)S(1)}, s32[]{:S(2)}) async-start(s8[14680064]{0:T(1024)(128)(4,1)} %bitcast.60), calls=%async_computation.7 | async-start | bytes 8388608 | tf_op jit(solution)/shard_map/while
  441.8 15.2 %slice-start.3 = ((s8[14680064]{0:T(1024)(128)(4,1)}), s8[2097152]{0:T(1024)(128)(4,1)S(1)}, s32[]{:S(2)}) async-start(s8[14680064]{0:T(1024)(128)(4,1)} %bitcast.60), calls=%async_computation.8 | async-start | bytes 4194304 | tf_op jit(solution)/shard_map/while
  441.8 20.4 %slice-start.8 = ((s8[7340032]{0:T(1024)(128)(4,1)}), s8[4194304]{0:T(1024)(128)(4,1)S(1)}, s32[]{:S(2)}) async-start(s8[7340032]{0:T(1024)(128)(4,1)} %bitcast.65), calls=%async_computation.13 | async-start | bytes 8388608 | tf_op jit(solution)/shard_map/while
  462.2 13.0 %copy-start = (f32[3584,1024]{1,0:T(8,128)}, f32[3584,1024]{1,0:T(8,128)S(1)}, u32[]{:S(2)}) copy-start(f32[3584,1024]{1,0:T(8,128)S(1)} %select_add_fusion.6) | copy-start | bytes 44040196 | tf_op jit(solution)/shard_map/while
  489.0 13.0 %copy-start.2 = (bf16[128,1024]{1,0:T(8,128)(2,1)}, bf16[128,1024]{1,0:T(8,128)(2,1)S(1)}, u32[]{:S(2)}) copy-start(bf16[128,1024]{1,0:T(8,128)(2,1)S(1)} %get-tuple-element.380) | copy-start | bytes 786436 | tf_op jit(solution)/shard_map/while
  501.9 15.2 %slice-start = ((s8[14680064]{0:T(1024)(128)(4,1)}), s8[4194304]{0:T(1024)(128)(4,1)S(1)}, s32[]{:S(2)}) async-start(s8[14680064]{0:T(1024)(128)(4,1)} %bitcast.60), calls=%async_computation.5 | async-start | bytes 8388608 | tf_op jit(solution)/shard_map/while
  501.9 15.2 %slice-start.1 = ((s8[14680064]{0:T(1024)(128)(4,1)}), s8[4194304]{0:T(1024)(128)(4,1)S(1)}, s32[]{:S(2)}) async-start(s8[14680064]{0:T(1024)(128)(4,1)} %bitcast.60), calls=%async_computation.6 | async-start | bytes 8388608 | tf_op jit(solution)/shard_map/while
  501.9 15.2 %slice-start.2 = ((s8[14680064]{0:T(1024)(128)(4,1)}), s8[4194304]{0:T(1024)(128)(4,1)S(1)}, s32[]{:S(2)}) async-start(s8[14680064]{0:T(1024)(128)(4,1)} %bitcast.60), calls=%async_computation.7 | async-start | bytes 8388608 | tf_op jit(solution)/shard_map/while
  501.9 15.2 %slice-start.3 = ((s8[14680064]{0:T(1024)(128)(4,1)}), s8[2097152]{0:T(1024)(128)(4,1)S(1)}, s32[]{:S(2)}) async-start(s8[14680064]{0:T(1024)(128)(4,1)} %bitcast.60), calls=%async_computation.8 | async-start | bytes 4194304 | tf_op jit(solution)/shard_map/while
  501.9 20.4 %slice-start.8 = ((s8[7340032]{0:T(1024)(128)(4,1)}), s8[4194304]{0:T(1024)(128)(4,1)S(1)}, s32[]{:S(2)}) async-start(s8[7340032]{0:T(1024)(128)(4,1)} %bitcast.65), calls=%async_computation.13 | async-start | bytes 8388608 | tf_op jit(solution)/shard_map/while
  522.3 13.0 %copy-start = (f32[3584,1024]{1,0:T(8,128)}, f32[3584,1024]{1,0:T(8,128)S(1)}, u32[]{:S(2)}) copy-start(f32[3584,1024]{1,0:T(8,128)S(1)} %select_add_fusion.6) | copy-start | bytes 44040196 | tf_op jit(solution)/shard_map/while
  549.1 13.0 %copy-start.2 = (bf16[128,1024]{1,0:T(8,128)(2,1)}, bf16[128,1024]{1,0:T(8,128)(2,1)S(1)}, u32[]{:S(2)}) copy-start(bf16[128,1024]{1,0:T(8,128)(2,1)S(1)} %get-tuple-element.380) | copy-start | bytes 786436 | tf_op jit(solution)/shard_map/while
  562.1 15.2 %slice-start = ((s8[14680064]{0:T(1024)(128)(4,1)}), s8[4194304]{0:T(1024)(128)(4,1)S(1)}, s32[]{:S(2)}) async-start(s8[14680064]{0:T(1024)(128)(4,1)} %bitcast.60), calls=%async_computation.5 | async-start | bytes 8388608 | tf_op jit(solution)/shard_map/while
  562.1 15.2 %slice-start.1 = ((s8[14680064]{0:T(1024)(128)(4,1)}), s8[4194304]{0:T(1024)(128)(4,1)S(1)}, s32[]{:S(2)}) async-start(s8[14680064]{0:T(1024)(128)(4,1)} %bitcast.60), calls=%async_computation.6 | async-start | bytes 8388608 | tf_op jit(solution)/shard_map/while
  562.1 15.2 %slice-start.2 = ((s8[14680064]{0:T(1024)(128)(4,1)}), s8[4194304]{0:T(1024)(128)(4,1)S(1)}, s32[]{:S(2)}) async-start(s8[14680064]{0:T(1024)(128)(4,1)} %bitcast.60), calls=%async_computation.7 | async-start | bytes 8388608 | tf_op jit(solution)/shard_map/while
  562.1 15.2 %slice-start.3 = ((s8[14680064]{0:T(1024)(128)(4,1)}), s8[2097152]{0:T(1024)(128)(4,1)S(1)}, s32[]{:S(2)}) async-start(s8[14680064]{0:T(1024)(128)(4,1)} %bitcast.60), calls=%async_computation.8 | async-start | bytes 4194304 | tf_op jit(solution)/shard_map/while
  562.1 20.4 %slice-start.8 = ((s8[7340032]{0:T(1024)(128)(4,1)}), s8[4194304]{0:T(1024)(128)(4,1)S(1)}, s32[]{:S(2)}) async-start(s8[7340032]{0:T(1024)(128)(4,1)} %bitcast.65), calls=%async_computation.13 | async-start | bytes 8388608 | tf_op jit(solution)/shard_map/while
  582.5 13.0 %copy-start = (f32[3584,1024]{1,0:T(8,128)}, f32[3584,1024]{1,0:T(8,128)S(1)}, u32[]{:S(2)}) copy-start(f32[3584,1024]{1,0:T(8,128)S(1)} %select_add_fusion.6) | copy-start | bytes 44040196 | tf_op jit(solution)/shard_map/while
  609.3 13.0 %copy-start.2 = (bf16[128,1024]{1,0:T(8,128)(2,1)}, bf16[128,1024]{1,0:T(8,128)(2,1)S(1)}, u32[]{:S(2)}) copy-start(bf16[128,1024]{1,0:T(8,128)(2,1)S(1)} %get-tuple-element.380) | copy-start | bytes 786436 | tf_op jit(solution)/shard_map/while
  622.2 15.2 %slice-start = ((s8[14680064]{0:T(1024)(128)(4,1)}), s8[4194304]{0:T(1024)(128)(4,1)S(1)}, s32[]{:S(2)}) async-start(s8[14680064]{0:T(1024)(128)(4,1)} %bitcast.60), calls=%async_computation.5 | async-start | bytes 8388608 | tf_op jit(solution)/shard_map/while
  622.2 15.2 %slice-start.1 = ((s8[14680064]{0:T(1024)(128)(4,1)}), s8[4194304]{0:T(1024)(128)(4,1)S(1)}, s32[]{:S(2)}) async-start(s8[14680064]{0:T(1024)(128)(4,1)} %bitcast.60), calls=%async_computation.6 | async-start | bytes 8388608 | tf_op jit(solution)/shard_map/while
  622.2 15.2 %slice-start.2 = ((s8[14680064]{0:T(1024)(128)(4,1)}), s8[4194304]{0:T(1024)(128)(4,1)S(1)}, s32[]{:S(2)}) async-start(s8[14680064]{0:T(1024)(128)(4,1)} %bitcast.60), calls=%async_computation.7 | async-start | bytes 8388608 | tf_op jit(solution)/shard_map/while
  622.3 15.2 %slice-start.3 = ((s8[14680064]{0:T(1024)(128)(4,1)}), s8[2097152]{0:T(1024)(128)(4,1)S(1)}, s32[]{:S(2)}) async-start(s8[14680064]{0:T(1024)(128)(4,1)} %bitcast.60), calls=%async_computation.8 | async-start | bytes 4194304 | tf_op jit(solution)/shard_map/while
  622.3 20.4 %slice-start.8 = ((s8[7340032]{0:T(1024)(128)(4,1)}), s8[4194304]{0:T(1024)(128)(4,1)S(1)}, s32[]{:S(2)}) async-start(s8[7340032]{0:T(1024)(128)(4,1)} %bitcast.65), calls=%async_computation.13 | async-start | bytes 8388608 | tf_op jit(solution)/shard_map/while
  642.6 13.0 %copy-start = (f32[3584,1024]{1,0:T(8,128)}, f32[3584,1024]{1,0:T(8,128)S(1)}, u32[]{:S(2)}) copy-start(f32[3584,1024]{1,0:T(8,128)S(1)} %select_add_fusion.6) | copy-start | bytes 44040196 | tf_op jit(solution)/shard_map/while
  678.0 47.1 %collective-permute-start.2 = (bf16[1024,3584]{1,0:T(8,128)(2,1)}, bf16[1024,3584]{1,0:T(8,128)(2,1)}, u32[]{:S(2)}, u32[]{:S(2)}) collective-permute-start(bf16[1024,3584]{1,0:T(8,128)(2,1)} %convert_element_type.124), channel_id=1, source_target_pairs={{0,1},{1,0},{2,3},{3,2},{4,5},{5,4},{6,7},{7,6},{8,9},{9,8},{10,11... | collective-permute-start | bytes 22020104 | tf_op jit(solution)/shard_map/ppermute | solution.py:8
  687.4 48.8 %collective-permute-start.1 = (bf16[3584,1024]{1,0:T(8,128)(2,1)}, bf16[3584,1024]{1,0:T(8,128)(2,1)}, u32[]{:S(2)}, u32[]{:S(2)}) collective-permute-start(bf16[3584,1024]{1,0:T(8,128)(2,1)} %convert_element_type.121), channel_id=1, source_target_pairs={{0,1},{1,0},{2,3},{3,2},{4,5},{5,4},{6,7},{7,6},{8,9},{9,8},{10,11... | collective-permute-start | bytes 22020104 | tf_op jit(solution)/shard_map/ppermute | solution.py:8
  688.6 15.9 %all-to-all-start.4 = ((bf16[32,1,22]{2,1,0:T(2,128)(2,1)}), bf16[32,1,22]{2,1,0:T(2,128)(2,1)S(1)}, u32[]{:S(2)}, u32[]{:S(2)}) async-start(bf16[32,1,22]{2,1,0:T(2,128)(2,1)} %convert_element_type.135), calls=%async_computation.4 | async-start | bytes 32768 | tf_op jit(solution)/shard_map/all_to_all | solution.py:127
  704.5 128.5 %all-to-all-start.3 = ((bf16[32,22,3584]{2,1,0:T(8,128)(2,1)}), bf16[32,22,3584]{2,1,0:T(8,128)(2,1)}, u32[]{:S(2)}, u32[]{:S(2)}) async-start(bf16[32,22,3584]{2,1,0:T(8,128)(2,1)} %reshape.204), calls=%async_computation.3 | async-start | bytes 11010048 | tf_op jit(solution)/shard_map/all_to_all | solution.py:124
  719.9 28.1 %collective-permute-start = (bf16[3584,1024]{1,0:T(8,128)(2,1)}, bf16[3584,1024]{1,0:T(8,128)(2,1)}, u32[]{:S(2)}, u32[]{:S(2)}) collective-permute-start(bf16[3584,1024]{1,0:T(8,128)(2,1)} %convert_element_type.118), channel_id=1, source_target_pairs={{0,1},{1,0},{2,3},{3,2},{4,5},{5,4},{6,7},{7,6},{8,9},{9,8},{10,11... | collective-permute-start | bytes 22020104 | tf_op jit(solution)/shard_map/ppermute | solution.py:8
  725.1 22.9 %slice-start.4 = ((s8[14680064]{0:T(1024)(128)(4,1)}), s8[4194304]{0:T(1024)(128)(4,1)S(1)}, s32[]{:S(2)}) async-start(s8[14680064]{0:T(1024)(128)(4,1)} %bitcast.62), calls=%async_computation.9 | async-start | bytes 8388608
  725.1 22.9 %slice-start.5 = ((s8[14680064]{0:T(1024)(128)(4,1)}), s8[4194304]{0:T(1024)(128)(4,1)S(1)}, s32[]{:S(2)}) async-start(s8[14680064]{0:T(1024)(128)(4,1)} %bitcast.62), calls=%async_computation.10 | async-start | bytes 8388608
  (52 other events, 390.8 us)
where the time goes:
time: 881 us; the launch traced here: 871 us
  matrix products  349 us (40%)
  waiting for transfers between devices  297 us (34%)
  local copies, waits for them, and re-layouts  113 us (13%)
  other arithmetic  71.4 us (8%)
  starting transfers between devices  26.8 us (3%)
  loops' own time  12.2 us (1%)
    dot_general x36, matrix products, contract(): lax.dot_general(left, right, (((left_dim,), (right_dim,)), ((), ())), pre...  304 us
    all_to_all x1, waiting for transfers between devices, shards(): lax.all_to_all(pack(tokens), 'expert', split_axis=0, concat_axis=0, tiled...  110 us
    all_to_all x1, waiting for transfers between devices, shards(): lax.all_to_all(pack(cotangent), 'expert', split_axis=0, concat_axis=0, ti...  109 us
    all_to_all x1, waiting for transfers between devices, shards(): lax.all_to_all(summed.astype(jnp.bfloat16), 'expert', split_axis=0, conca...  77.4 us
  transfers between devices with their start and end apart: 8, of which 3 were waited for; matrix products, arithmetic and copies ran while one was open for 12% of the time, Pallas kernels for 0%

commit v1 on v0

v1 whole, which is shorter than its diff:
```python
import functools

import jax
import jax.numpy as jnp
from jax import lax
from jax.experimental import pallas as pl
from jax.experimental.pallas import tpu as pltpu
from jax.sharding import PartitionSpec as P

PLANE = 8
LANES = 128
BF16 = jnp.bfloat16
F32 = jnp.float32
VMEM_BYTES = 60 * 1024 * 1024


def silu_parts(gate):
    sig = jax.nn.sigmoid(gate)
    return (gate * sig, sig * (1.0 + gate * (1.0 - sig)))


def contract(left, right, left_dim, right_dim):
    return lax.dot_general(
        left, right, (((left_dim,), (right_dim,)), ((), ())), preferred_element_type=jnp.float32
    )


def column_tile(width):
    return width // 7 if width % (7 * LANES) == 0 else LANES


def remote(src, dst, send_sem, recv_sem, device):
    return pltpu.make_async_remote_copy(
        src_ref=src,
        dst_ref=dst,
        send_sem=send_sem,
        recv_sem=recv_sem,
        device_id={"expert": device},
        device_id_type=pl.DeviceIdType.MESH,
    )


def greet(planes, z, p):
    barrier = pltpu.get_barrier_semaphore()
    for j in range(1, PLANE):
        pl.semaphore_signal(
            barrier,
            inc=1,
            device_id={"expert": z * PLANE + (p + j) % PLANE},
            device_id_type=pl.DeviceIdType.MESH,
        )
    for k in range(1, planes):
        pl.semaphore_signal(
            barrier,
            inc=1,
            device_id={"expert": (z + k) % planes * PLANE + p},
            device_id_type=pl.DeviceIdType.MESH,
        )
    pl.semaphore_wait(barrier, PLANE - 1 + planes - 1)


def one_hot_rows(codes, weights, cap):
    seat = lax.broadcasted_iota(jnp.int32, (cap, codes.shape[1]), 0).astype(F32)
    parts = []
    for q in range(PLANE):
        parts.append(jnp.where(seat == codes[q : q + 1, :], weights[q : q + 1, :], 0.0))
    return jnp.concatenate(parts, axis=0).astype(BF16)


def dispatch_kernel(
    planes, meta_ref, x_ref, dy_ref, rx, rdy, gm_out, gm, gx, gdy, sx, sdy, msend, mrecv,
    zsend, zrecv, psend, precv, lsem
):
    me = lax.axis_index("expert")
    z, p = me // PLANE, me % PLANE
    cap = rx.shape[1]
    width = x_ref.shape[1]
    tile = column_tile(width)
    greet(planes, z, p)

    def meta_copy(k):
        there = (z + k) % planes
        return remote(
            meta_ref.at[there], gm.at[z], msend.at[k], mrecv.at[z], there * PLANE + p
        )

    for k in range(1, planes):
        meta_copy(k).start()

    def chain_copy(which, up, src, ref):
        held = (gx, gdy)[which]
        there = z + 1 if up else z - 1
        return remote(
            ref, held.at[src], zsend.at[which, up, src], zrecv.at[which, src], there * PLANE + p
        )

    def chain_goes(up, src):
        return (src <= z) & (z < planes - 1) if up else (src >= z) & (z > 0)

    def forward(which, src, ref):
        for up in (0, 1):

            @pl.when(chain_goes(up, src))
            def _():
                chain_copy(which, up, src, ref).start()

    def plane_copy(which, src, j):
        packed, out = ((sx, rx), (sdy, rdy))[which]
        q = (p + j) % PLANE
        return remote(
            packed.at[src, q],
            out.at[src * PLANE + p],
            psend.at[which, src, j],
            precv.at[which, src, j],
            z * PLANE + q,
        )

    def own_copy(which, src):
        packed, out = ((sx, rx), (sdy, rdy))[which]
        return pltpu.make_async_copy(
            packed.at[src, p], out.at[src * PLANE + p], lsem.at[which, src]
        )

    def pack(which, src, ref):
        packed = (sx, sdy)[which]
        codes = gm[src, 0:PLANE, :]
        weights = gm[src, PLANE : 2 * PLANE, :] if which else jnp.ones_like(codes)
        rows = one_hot_rows(codes, weights, cap)

        @pl.loop(0, width // tile)
        def _(c):
            cols = pl.ds(pl.multiple_of(c * tile, tile), tile)
            got = jnp.dot(rows, ref[:, cols], preferred_element_type=F32)
            for q in range(PLANE):
                packed[src, q, :, cols] = got[q * cap : (q + 1) * cap].astype(BF16)

        for j in range(1, PLANE):
            plane_copy(which, src, j).start()
        own_copy(which, src).start()

    forward(0, z, x_ref)
    forward(1, z, dy_ref)
    gm[z] = meta_ref[z]
    pack(0, z, x_ref)
    pack(1, z, dy_ref)

    @pl.loop(0, 2 * (planes - 1))
    def _(i):
        away = (i // 2 + 1) * (1 - 2 * (i % 2))
        src = z - away

        @pl.when((src >= 0) & (src < planes))
        def _():
            remote(gm.at[src], gm.at[src], msend.at[0], mrecv.at[src], me).wait_recv()
            for which in (0, 1):
                held = (gx, gdy)[which]
                remote(
                    held.at[src], held.at[src], zsend.at[which, 0, src], zrecv.at[which, src], me
                ).wait_recv()
                forward(which, src, held.at[src])
                pack(which, src, held.at[src])

    gm_out[...] = gm[...]
    for k in range(1, planes):
        meta_copy(k).wait_send()

    @pl.loop(0, planes)
    def _(src):
        for which in (0, 1):
            for up in (0, 1):

                @pl.when(chain_goes(up, src))
                def _():
                    held = (gx, gdy)[which]
                    chain_copy(which, up, src, held.at[src]).wait_send()

            for j in range(1, PLANE):
                copy = plane_copy(which, src, j)
                copy.wait_send()
                copy.wait_recv()
            own_copy(which, src).wait()


def dispatch(meta, tokens, cotangent, slots, cap):
    planes = slots // PLANE
    tok, width = tokens.shape
    vmem = pl.BlockSpec(memory_space=pltpu.VMEM)
    anywhere = pl.BlockSpec(memory_space=pl.ANY)
    return pl.pallas_call(
        functools.partial(dispatch_kernel, planes),
        out_shape=(
            jax.ShapeDtypeStruct((slots, cap, width), BF16),
            jax.ShapeDtypeStruct((slots, cap, width), BF16),
            jax.ShapeDtypeStruct((planes, 2 * PLANE, tok), F32),
        ),
        in_specs=[vmem] * 3,
        out_specs=(anywhere, anywhere, vmem),
        scratch_shapes=[
            pltpu.VMEM((planes, 2 * PLANE, tok), F32),
            pltpu.VMEM((planes, tok, width), BF16),
            pltpu.VMEM((planes, tok, width), BF16),
            pltpu.VMEM((planes, PLANE, cap, width), BF16),
            pltpu.VMEM((planes, PLANE, cap, width), BF16),
            pltpu.SemaphoreType.DMA((planes,)),
            pltpu.SemaphoreType.DMA((planes,)),
            pltpu.SemaphoreType.DMA((2, 2, planes)),
            pltpu.SemaphoreType.DMA((2, planes)),
            pltpu.SemaphoreType.DMA((2, planes, PLANE)),
            pltpu.SemaphoreType.DMA((2, planes, PLANE)),
            pltpu.SemaphoreType.DMA((2, planes)),
        ],
        compiler_params=pltpu.CompilerParams(
            collective_id=0, has_side_effects=True, vmem_limit_bytes=VMEM_BYTES
        ),
    )(meta, tokens, cotangent)


def combine_kernel(
    planes, piece, gm_ref, dx_ref, found_ref, rp, sp, rs, psend, precv, lsem, zsend, zrecv
):
    me = lax.axis_index("expert")
    z, p = me // PLANE, me % PLANE
    cap, wide = piece.shape[1], piece.shape[2]
    width = wide - LANES
    greet(planes, z, p)
    order = sorted(range(planes), key=lambda k: -min(k, planes - k))

    def plane_copy(b, j):
        q = (p + j) % PLANE
        return remote(
            piece.at[b * PLANE + q], rp.at[b, p], psend.at[b, j], precv.at[b, j], z * PLANE + q
        )

    def own_copy(b):
        return pltpu.make_async_copy(piece.at[b * PLANE + p], rp.at[b, p], lsem.at[b])

    def home_copy(b):
        return remote(sp.at[b], rs.at[z], zsend.at[b], zrecv.at[z], b * PLANE + p)

    for k in order:
        b = (z + k) % planes
        for j in range(1, PLANE):
            plane_copy(b, j).start()
        own_copy(b).start()

    def partial(b, rows, cols):
        parts = [rp[b, q, :, cols].astype(F32) for q in range(PLANE)]
        return contract(rows, jnp.concatenate(parts, axis=0).astype(BF16), 0, 0)

    def arrived(b):
        for j in range(1, PLANE):
            plane_copy(b, j).wait_recv()
        own_copy(b).wait()
        codes = gm_ref[b, 0:PLANE, :]
        return one_hot_rows(codes, jnp.ones_like(codes), cap)

    tile = column_tile(width)

    for k in order[:-1]:
        b = (z + k) % planes
        rows = arrived(b)

        @pl.loop(0, width // tile)
        def _(c):
            cols = pl.ds(pl.multiple_of(c * tile, tile), tile)
            sp[b, :, cols] = partial(b, rows, cols).astype(BF16)

        sp[b, :, width:wide] = partial(b, rows, slice(width, wide)).astype(BF16)
        home_copy(b).start()

    own_rows = arrived(z)
    for k in order[:-1]:
        src = (z + k) % planes
        remote(rs.at[src], rs.at[src], zsend.at[src], zrecv.at[src], me).wait_recv()

    def total(cols):
        acc = partial(z, own_rows, cols)
        for k in order[:-1]:
            acc = acc + rs[(z + k) % planes, :, cols].astype(F32)
        return acc

    @pl.loop(0, width // tile)
    def _(c):
        cols = pl.ds(pl.multiple_of(c * tile, tile), tile)
        dx_ref[:, cols] = total(cols).astype(BF16)

    found_ref[...] = total(slice(width, wide))

    for k in order:
        b = (z + k) % planes
        for j in range(1, PLANE):
            plane_copy(b, j).wait_send()
    for k in order[:-1]:
        home_copy((z + k) % planes).wait_send()


def combine(piece, gm, tok):
    slots, cap, wide = piece.shape
    planes = slots // PLANE
    vmem = pl.BlockSpec(memory_space=pltpu.VMEM)
    anywhere = pl.BlockSpec(memory_space=pl.ANY)
    return pl.pallas_call(
        functools.partial(combine_kernel, planes),
        out_shape=(
            jax.ShapeDtypeStruct((tok, wide - LANES), BF16),
            jax.ShapeDtypeStruct((tok, LANES), F32),
        ),
        in_specs=[anywhere, vmem],
        out_specs=(vmem, vmem),
        scratch_shapes=[
            pltpu.VMEM((planes, PLANE, cap, wide), BF16),
            pltpu.VMEM((planes, tok, wide), BF16),
            pltpu.VMEM((planes, tok, wide), BF16),
            pltpu.SemaphoreType.DMA((planes, PLANE)),
            pltpu.SemaphoreType.DMA((planes, PLANE)),
            pltpu.SemaphoreType.DMA((planes,)),
            pltpu.SemaphoreType.DMA((planes,)),
            pltpu.SemaphoreType.DMA((planes,)),
        ],
        compiler_params=pltpu.CompilerParams(
            collective_id=1, has_side_effects=True, vmem_limit_bytes=VMEM_BYTES
        ),
    )(piece, gm)


def shards(tokens, cotangent, expert_ids, gate_probs, slot_expert, w_gate, w_up, w_down):
    slots = lax.axis_size("expert")
    here = lax.axis_index("expert")
    planes = slots // PLANE
    tok_rows, quarter = tokens.shape
    top = expert_ids.shape[1]
    experts = slots - max(2, slots // 8)
    capacity = max(2, 5 * tok_rows * top // (4 * experts))
    capacity = (capacity + 7) // 8 * 8
    width = w_gate.shape[1]
    total = slots * capacity
    hit = expert_ids[:, :, None] == slot_expert[None, None, :]
    probs = gate_probs.astype(F32)
    hits = hit.astype(F32)
    taken = jnp.sum(hits, axis=1)
    weight = jnp.sum(hits * probs[:, :, None], axis=1)
    row = jnp.arange(tok_rows, dtype=jnp.int32)
    earlier = (row[:, None] > row[None, :]).astype(BF16)
    rank = jnp.dot(earlier, taken.astype(BF16), preferred_element_type=F32)
    code = jnp.where(taken > 0.0, rank, -1.0)
    meta = jnp.concatenate(
        [code.T.reshape(planes, PLANE, tok_rows), weight.T.reshape(planes, PLANE, tok_rows)],
        axis=1,
    )
    part_x, part_dy, got_meta = dispatch(meta, tokens, cotangent, slots, capacity)
    xs = lax.all_gather(part_x, "dp", axis=2, tiled=True).reshape(total, width)
    d_out = lax.all_gather(part_dy, "dp", axis=2, tiled=True).reshape(total, width)
    wg = w_gate[0]
    wu = w_up[0]
    wd = w_down[0]
    gate = contract(xs, wg, 1, 0)
    up = contract(xs, wu, 1, 0)
    d_hidden = contract(d_out, wd, 1, 1)
    act, slope = silu_parts(gate)
    hidden = (act * up).astype(BF16)
    score = jnp.sum(hidden.astype(F32) * d_hidden, axis=1)
    d_gate_pre = (d_hidden * up * slope).astype(BF16)
    d_up_pre = (d_hidden * act).astype(BF16)
    piece = contract(d_gate_pre, wg, 1, 1) + contract(d_up_pre, wu, 1, 1)
    summed = lax.psum_scatter(
        piece.astype(BF16).reshape(slots, capacity, width),
        "dp",
        scatter_dimension=2,
        tiled=True,
    )
    scores = lax.psum(score.reshape(slots, capacity), "dp").astype(BF16)
    lane = jnp.arange(LANES, dtype=jnp.int32)
    placed_scores = jnp.where(lane == here, scores[:, :, None], 0.0).astype(BF16)
    slot = jnp.arange(slots, dtype=jnp.int32)
    repeat = (slot_expert[:, None] == slot_expert[None, :]) & (slot[:, None] > slot[None, :])
    first = jnp.logical_not(jnp.any(repeat, axis=1))
    plane_first = lax.dynamic_slice_in_dim(first, here // PLANE * PLANE, PLANE, 0)
    back_code = jnp.where(plane_first[None, :, None], got_meta[:, :PLANE], -1.0)
    d_tokens, found = combine(
        jnp.concatenate([summed, placed_scores], axis=2), back_code, tok_rows
    )
    grad_down = contract(hidden, d_out, 0, 0).astype(BF16)[None]
    grad_gate = contract(xs, d_gate_pre, 0, 0).astype(BF16)[None]
    grad_up = contract(xs, d_up_pre, 0, 0).astype(BF16)[None]
    listed = jnp.where(hit & first[None, None, :], found[:, None, :slots], 0.0)
    d_probs = jnp.sum(listed, axis=2) / probs
    return (d_tokens, d_probs, grad_gate, grad_up, grad_down)


def solution(mesh):
    placed = (
        P("expert", "dp"),
        P("expert", "dp"),
        P("expert", None),
        P("expert", None),
        P(),
        P("expert", None, "dp"),
        P("expert", None, "dp"),
        P("expert", "dp", None),
    )
    return jax.shard_map(
        shards,
        mesh=mesh,
        in_specs=placed,
        out_specs=(
            P("expert", "dp"),
            P("expert", None),
            P("expert", None, "dp"),
            P("expert", None, "dp"),
            P("expert", "dp", None),
        ),
        check_vma=False,
    )
```

time: 881 us -> 341 us (0.39); the launches traced: 871 us -> 341 us
  waiting for transfers between devices: 297 us -> 0 us
  matrix products: 349 us -> 73.7 us
  Pallas kernels: 0 us -> 253 us
  local copies, waits for them, and re-layouts: 113 us -> 2.06 us
  other arithmetic: 71.4 us -> 10.7 us
  starting transfers between devices: 26.8 us -> 0 us
  loops' own time: 12.2 us -> 0 us
    all_to_all x5 -> x0, waiting for transfers between devices: 297 us -> none  [the longest x1 110 us: shards(): lax.all_to_all(pack(tokens), 'expert', split_axis=0, concat_axis=0, tiled...]
    pallas_call x0 -> x2, Pallas kernels: none -> 253 us  [the longest x1 146 us: dispatch(): pl.pallas_call(functools.partial(dispatch_kernel, planes), out_shape=(jax...]
    dot_general x36 -> x8, matrix products: 304 us -> 73.6 us  [contract(): lax.dot_general(left, right, (((left_dim,), (right_dim,)), ((), ())), pre...]
    reshape x10 -> x0, local copies, waits for them, and re-layouts: 55.3 us -> none  [the longest x2 17.1 us: shards(): back_x.reshape(total, quarter)[flat_pos].reshape(tok_rows, top, quarter)]
    dot_general x18 -> x1, matrix products: 44.6 us -> 0.14 us  [shards(): rank = jnp.dot(earlier, taken.astype(BF16), preferred_element_type=F32)]
    broadcast_in_dim x3 -> x0, other arithmetic: 30.5 us -> none  [the longest x1 11.7 us: shards(): grad_up = (acc_up + jnp.where(same, got_up, 0.0)).astype(jnp.bfloat16)[None]]
    convert_element_type x12 -> x1, other arithmetic: 29.1 us -> 0.69 us  [shards(): probs = gate_probs.astype(F32)]
    all_to_all x5 -> x0, starting transfers between devices: 26.1 us -> none  [the longest x1 7.3 us: shards(): lax.all_to_all(send_probs, 'expert', split_axis=0, concat_axis=0, tiled=T...]
  transfers between devices with their start and end apart: 8 -> 0, of which waited for: 3 -> 0; matrix products, arithmetic and copies ran while one was open for 12% -> 0% of each run, Pallas kernels for 0% -> 0%
where the time goes in v1:
time: 341 us
  Pallas kernels  253 us (74%)
  matrix products  73.7 us (22%)
  other arithmetic  10.7 us (3%)
    pallas_call x1, Pallas kernels, dispatch(): pl.pallas_call(functools.partial(dispatch_kernel, planes), out_shape=(jax...  146 us
    pallas_call x1, Pallas kernels, combine(): pl.pallas_call(functools.partial(combine_kernel, planes), out_shape=(jax....  107 us
    dot_general x8, matrix products, contract(): lax.dot_general(left, right, (((left_dim,), (right_dim,)), ((), ())), pre...  73.6 us

profile of v1, /device:TPU:0, one launch (start us, length us, event | category | flops | bytes accessed | tf_op | source)
XLA Modules:
  0.0 340.5 jit_solution(16495502269279873183)
XLA Ops:
  0.7 0.9 fusion.20
  1.6 0.1 dynamic_slice.3
  1.7 0.7 convert_element_type.48
  2.3 0.8 fusion.17
  3.1 0.1 fusion.16
  3.2 0.6 pad_maximum_fusion.1.meta_ref
  3.9 146.1 %shard_map.119 = (bf16[32,24,3584]{2,1,0:T(8,128)(2,1)}, bf16[32,24,3584]{2,1,0:T(8,128)(2,1)}, f32[4,16,128]{2,1,0:T(8,128)}) custom-call(f32[4,16,128]{2,1,0:T(8,128)} %pad_maximum_fusion.1.meta_ref, bf16[128,3584]{1,0:T(8,128)(2,1)} %x_ref.1, bf16[128,3584]{1,0:T(8,128)(2,1)} %dy_ref.1), custom_call_target="tpu_custom_call" | custom-call | tf_op jit(solution)/shard_map/pallas_call | solution.py:189
  150.0 1.4 slice_select_fusion.gm_ref
  151.4 0.0 copy-start.4
  151.4 0.0 copy-start.5
  151.4 0.0 slice-start
  151.4 9.8 %fusion.2 = f32[768,1024]{1,0:T(8,128)S(1)} fusion(bf16[768,3584]{1,0:T(8,128)(2,1)} %bitcast.56, bf16[1,3584,1024]{2,1,0:T(8,128)(2,1)} %param.13), kind=kOutput, calls=%fused_computation.6 | convolution fusion | flops 5637144576 | bytes 15990784 | tf_op jit(solution)/shard_map/dot_general | solution.py:23
  161.3 0.0 copy-done.4
  161.3 0.0 copy-done.5
  161.3 0.0 slice-start.1
  161.3 0.0 slice-start.2
  161.3 7.5 %fusion.6 = f32[768,1024]{1,0:T(8,128)} fusion(bf16[768,3584]{1,0:T(8,128)(2,1)S(1)} %bitcast.58, bf16[1,3584,1024]{2,1,0:T(8,128)(2,1)S(1)} %copy-done.4), kind=kOutput, calls=%fused_computation.10 | convolution fusion | flops 5637144576 | bytes 15990784 | tf_op jit(solution)/shard_map/dot_general | solution.py:23
  168.8 0.0 slice-done
  168.8 0.0 slice-done.1
  168.8 0.0 slice-start.3
  168.8 11.9 %multiply_reduce_fusion = (bf16[768]{0:T(1024)(128)(2,1)S(1)}, bf16[768,1024]{1,0:T(8,128)(2,1)S(1)}, bf16[768,1024]{1,0:T(8,128)(2,1)}, bf16[768,1024]{1,0:T(8,128)(2,1)}) fusion(f32[768,1024]{1,0:T(8,128)} %fusion.6, f32[768,1024]{1,0:T(8,128)S(1)} %fusion.2, bf16[768,3584]{1,0:T(8,128)(2,1)} %bitcast.52, bf16[1,1024,3584]{2,1,0:T(8,128)(2,1)S(1)} %bitcast.49), kind=kOutput, calls=%fused_computation.18 | convolution fusion | flops 5651299328 | bytes 23856640 | tf_op jit(solution)/shard_map/dot_general | solution.py:23
  180.7 0.0 slice-done.2
  180.7 0.0 slice-done.3
  180.7 7.3 %fusion = f32[768,3584]{1,0:T(8,128)S(1)} fusion(bf16[768,1024]{1,0:T(8,128)(2,1)} %get-tuple-element.19, bf16[1,3584,1024]{2,1,0:T(8,128)(2,1)S(1)} %bitcast.51), kind=kOutput, calls=%fused_computation.4 | convolution fusion | flops 5637144576 | bytes 19922944 | tf_op jit(solution)/shard_map/dot_general | solution.py:23
  188.1 10.3 %add_convert_fusion = bf16[768,3584]{1,0:T(8,128)(2,1)} fusion(f32[768,3584]{1,0:T(8,128)S(1)} %fusion, bf16[768,1024]{1,0:T(8,128)(2,1)} %get-tuple-element.20, bf16[1,3584,1024]{2,1,0:T(8,128)(2,1)} %param.14), kind=kOutput, calls=%fused_computation | convolution fusion | flops 5642649600 | bytes 25427968 | tf_op jit(solution)/shard_map/dot_general | solution.py:23
  198.4 0.1 convert_element_type.55
  198.5 0.2 broadcast_select_fusion
  198.6 5.5 %pad_maximum_fusion.piece = bf16[32,24,3712]{2,1,0:T(8,128)(2,1)} fusion(bf16[32,24,128]{2,1,0:T(8,128)(2,1)S(1)} %broadcast_select_fusion, bf16[32,24,3584]{2,1,0:T(8,128)(2,1)} %bitcast.45), kind=kLoop, calls=%fused_computation.17 | loop fusion | flops 11403264 | bytes 11403264 | tf_op jit(solution)/shard_map/concatenate | solution.py:380
  204.1 0.0 copy-start.1
  204.1 0.0 copy-start.3
  204.1 107.1 %shard_map.120 = (bf16[128,3584]{1,0:T(8,128)(2,1)}, f32[128,128]{1,0:T(8,128)}) custom-call(bf16[32,24,3712]{2,1,0:T(8,128)(2,1)} %pad_maximum_fusion.piece, f32[4,8,128]{2,1,0:T(8,128)} %slice_select_fusion.gm_ref), custom_call_target="tpu_custom_call" | custom-call | tf_op jit(solution)/shard_map/pallas_call | solution.py:302
  311.2 0.9 copy.17
  312.1 0.0 copy-done.1
  312.1 0.0 copy-done.3
  312.1 0.1 select_reduce_fusion
  312.2 0.0 copy-done.2
  312.2 0.6 convert_divide_fusion
  312.8 10.4 %fusion.12 = bf16[1,3584,1024]{2,1,0:T(8,128)(2,1)} fusion(bf16[768,3584]{1,0:T(8,128)(2,1)} %bitcast.57, bf16[768,1024]{1,0:T(8,128)(2,1)} %get-tuple-element.19), kind=kOutput, calls=%fused_computation.14 | convolution fusion | flops 5640814592 | bytes 14417920 | tf_op jit(solution)/shard_map/dot_general | solution.py:23
  323.1 0.0 slice-done.6
  323.2 0.0 slice-done.7
  323.2 0.0 copy-done.6
  323.2 0.0 slice-start.5
  323.2 8.3 %fusion.13 = bf16[1,3584,1024]{2,1,0:T(8,128)(2,1)} fusion(bf16[768,3584]{1,0:T(8,128)(2,1)S(1)} %bitcast.61, bf16[768,1024]{1,0:T(8,128)(2,1)S(1)} %copy-done.6), kind=kOutput, calls=%fused_computation.15 | convolution fusion | flops 5640814592 | bytes 14417920 | tf_op jit(solution)/shard_map/dot_general | solution.py:23
  331.5 0.0 slice-done.4
  331.5 0.0 slice-done.5
  331.5 8.1 %fusion.14 = bf16[1,1024,3584]{2,1,0:T(8,128)(2,1)} fusion(bf16[768,1024]{1,0:T(8,128)(2,1)S(1)} %get-tuple-element.18, bf16[768,3584]{1,0:T(8,128)(2,1)S(1)} %bitcast.55), kind=kOutput, calls=%fused_computation.16 | convolution fusion | flops 5640814592 | bytes 14417920 | tf_op jit(solution)/shard_map/dot_general | solution.py:23
  339.6 0.0 copy-done
  339.6 0.9 copy.19
  (12 shorter events, 0.0 us)
Async XLA Ops:
  151.4 9.9 %copy-start.4 = (bf16[1,3584,1024]{2,1,0:T(8,128)(2,1)S(1)}, bf16[1,3584,1024]{2,1,0:T(8,128)(2,1)}, u32[]{:S(2)}) copy-start(bf16[1,3584,1024]{2,1,0:T(8,128)(2,1)} %param.14) | copy-start | bytes 22020100
  151.4 9.9 %copy-start.5 = (bf16[32,24,3584]{2,1,0:T(8,128)(2,1)S(1)}, bf16[32,24,3584]{2,1,0:T(8,128)(2,1)}, u32[]{:S(2)}) copy-start(bf16[32,24,3584]{2,1,0:T(8,128)(2,1)} %get-tuple-element.11) | copy-start | bytes 16515076
  151.4 17.4 %slice-start = ((s8[7340032]{0:T(1024)(128)(4,1)}), s8[4194304]{0:T(1024)(128)(4,1)S(1)}, s32[]{:S(2)}) async-start(s8[7340032]{0:T(1024)(128)(4,1)} %bitcast.48), calls=%async_computation | async-start | bytes 8388608
  161.3 7.5 %slice-start.1 = ((s8[7340032]{0:T(1024)(128)(4,1)}), s8[3145728]{0:T(1024)(128)(4,1)S(1)}, s32[]{:S(2)}) async-start(s8[7340032]{0:T(1024)(128)(4,1)} %bitcast.48), calls=%async_computation.1 | async-start | bytes 6291456
  161.3 19.4 %slice-start.2 = ((s8[7340032]{0:T(1024)(128)(4,1)}), s8[4194304]{0:T(1024)(128)(4,1)S(1)}, s32[]{:S(2)}) async-start(s8[7340032]{0:T(1024)(128)(4,1)} %bitcast.50), calls=%async_computation.2 | async-start | bytes 8388608
  168.8 11.9 %slice-start.3 = ((s8[7340032]{0:T(1024)(128)(4,1)}), s8[3145728]{0:T(1024)(128)(4,1)S(1)}, s32[]{:S(2)}) async-start(s8[7340032]{0:T(1024)(128)(4,1)} %bitcast.50), calls=%async_computation.3 | async-start | bytes 6291456
  204.1 108.0 %copy-start.1 = (s32[128,4]{0,1:T(4,128)S(1)}, s32[128,4]{0,1:T(4,128)}, u32[]{:S(2)}) copy-start(s32[128,4]{0,1:T(4,128)} %param.10) | copy-start | bytes 6148
  204.1 108.0 %copy-start.3 = (s32[32]{0:T(128)S(1)}, s32[32]{0:T(128)}, u32[]{:S(2)}) copy-start(s32[32]{0:T(128)} %param.12) | copy-start | bytes 388
  204.1 108.1 %copy-start.2 = (bf16[128,4]{0,1:T(4,128)(2,1)S(1)}, bf16[128,4]{0,1:T(4,128)(2,1)}, u32[]{:S(2)}) copy-start(bf16[128,4]{0,1:T(4,128)(2,1)} %param.11) | copy-start | bytes 3076
  204.1 119.0 %slice-start.6 = ((s8[5505024]{0:T(1024)(128)(4,1)}), s8[1310720]{0:T(1024)(128)(4,1)S(1)}, s32[]{:S(2)}) async-start(s8[5505024]{0:T(1024)(128)(4,1)} %bitcast.59), calls=%async_computation.6 | async-start | bytes 2621440
  312.8 10.4 %slice-start.7 = ((s8[5505024]{0:T(1024)(128)(4,1)}), s8[4194304]{0:T(1024)(128)(4,1)S(1)}, s32[]{:S(2)}) async-start(s8[5505024]{0:T(1024)(128)(4,1)} %bitcast.59), calls=%async_computation.7 | async-start | bytes 8388608
  312.8 10.4 %copy-start.6 = (bf16[768,1024]{1,0:T(8,128)(2,1)S(1)}, bf16[768,1024]{1,0:T(8,128)(2,1)}, u32[]{:S(2)}) copy-start(bf16[768,1024]{1,0:T(8,128)(2,1)} %get-tuple-element.20) | copy-start | bytes 4718596
  312.8 18.7 %slice-start.4 = ((s8[5505024]{0:T(1024)(128)(4,1)}), s8[4194304]{0:T(1024)(128)(4,1)S(1)}, s32[]{:S(2)}) async-start(s8[5505024]{0:T(1024)(128)(4,1)} %bitcast.53), calls=%async_computation.4 | async-start | bytes 8388608
  323.2 8.3 %slice-start.5 = ((s8[5505024]{0:T(1024)(128)(4,1)}), s8[1310720]{0:T(1024)(128)(4,1)S(1)}, s32[]{:S(2)}) async-start(s8[5505024]{0:T(1024)(128)(4,1)} %bitcast.53), calls=%async_computation.5 | async-start | bytes 2621440
  331.5 8.1 %copy-start = (bf16[128,3584]{1,0:T(8,128)(2,1)S(1)}, bf16[128,3584]{1,0:T(8,128)(2,1)}, u32[]{:S(2)}) copy-start(bf16[128,3584]{1,0:T(8,128)(2,1)} %get-tuple-element.26) | copy-start | bytes 2752516

commit v2 on v1

v2 whole, which is shorter than its diff:
```python
import functools

import jax
import jax.numpy as jnp
from jax import lax
from jax.experimental import pallas as pl
from jax.experimental.pallas import tpu as pltpu
from jax.sharding import PartitionSpec as P

PLANE = 8
LANES = 128
BF16 = jnp.bfloat16
F32 = jnp.float32
VMEM_BYTES = 62 * 1024 * 1024


def silu_parts(gate):
    sig = jax.nn.sigmoid(gate)
    return (gate * sig, sig * (1.0 + gate * (1.0 - sig)))


def contract(left, right, left_dim, right_dim):
    return lax.dot_general(
        left, right, (((left_dim,), (right_dim,)), ((), ())), preferred_element_type=jnp.float32
    )


def column_tile(width):
    return width // 7 if width % (7 * LANES) == 0 else LANES


def remote(src, dst, send_sem, recv_sem, device):
    return pltpu.make_async_remote_copy(
        src_ref=src,
        dst_ref=dst,
        send_sem=send_sem,
        recv_sem=recv_sem,
        device_id={"expert": device},
        device_id_type=pl.DeviceIdType.MESH,
    )


def greet(planes, z, p):
    barrier = pltpu.get_barrier_semaphore()
    for j in range(1, PLANE):
        pl.semaphore_signal(
            barrier,
            inc=1,
            device_id={"expert": z * PLANE + (p + j) % PLANE},
            device_id_type=pl.DeviceIdType.MESH,
        )
    for k in range(1, planes):
        pl.semaphore_signal(
            barrier,
            inc=1,
            device_id={"expert": (z + k) % planes * PLANE + p},
            device_id_type=pl.DeviceIdType.MESH,
        )
    pl.semaphore_wait(barrier, PLANE - 1 + planes - 1)


def one_hot_rows(codes, weights, cap):
    seat = lax.broadcasted_iota(jnp.int32, (cap, codes.shape[1]), 0).astype(F32)
    parts = []
    for q in range(PLANE):
        parts.append(jnp.where(seat == codes[q : q + 1, :], weights[q : q + 1, :], 0.0))
    return jnp.concatenate(parts, axis=0).astype(BF16)


def gather_rows(ref, lead, cols):
    parts = [ref[lead * PLANE + q, :, cols].astype(F32) for q in range(PLANE)]
    return jnp.concatenate(parts, axis=0).astype(BF16)


def dispatch_kernel(planes, fused, *refs):
    if fused:
        meta_ref, x_ref, dy_ref, wg_hbm, wu_hbm, wd_hbm = refs[:6]
        ox, ody, gm_out, hid_out, dg_out, du_out, sc_out = refs[6:13]
        gm, gx, gdy, sx, sdy, rx, rdy, wg, wu, wd = refs[13:23]
        acc_g, acc_u, acc_h, st_hid, st_dg, st_du, st_sc = refs[23:30]
        msend, mrecv, zsend, zrecv, psend, precv, lsem, wsem, osem, dsem, xsem = refs[30:]
    else:
        meta_ref, x_ref, dy_ref, rx, rdy, gm_out, gm, gx, gdy, sx, sdy = refs[:11]
        msend, mrecv, zsend, zrecv, psend, precv, lsem, xsem = refs[11:]
    me = lax.axis_index("expert")
    z, p = me // PLANE, me % PLANE
    cap = rx.shape[1]
    width = x_ref.shape[1]
    tile = column_tile(width)
    block = PLANE * cap

    def in_copy(which):
        return pltpu.make_async_copy(
            (x_ref, dy_ref)[which], (gx, gdy)[which].at[z], xsem.at[which]
        )

    def weight_copy(k):
        return pltpu.make_async_copy(
            (wg_hbm, wu_hbm, wd_hbm)[k], (wg, wu, wd)[k], wsem.at[k]
        )

    in_copy(0).start()
    in_copy(1).start()
    greet(planes, z, p)

    def meta_copy(k):
        there = (z + k) % planes
        return remote(
            meta_ref.at[there], gm.at[z], msend.at[k], mrecv.at[z], there * PLANE + p
        )

    for k in range(1, planes):
        meta_copy(k).start()

    def chain_copy(which, up, src, ref):
        held = (gx, gdy)[which]
        there = z + 1 if up else z - 1
        return remote(
            ref, held.at[src], zsend.at[which, up, src], zrecv.at[which, src], there * PLANE + p
        )

    def chain_goes(up, src):
        return (src <= z) & (z < planes - 1) if up else (src >= z) & (z > 0)

    def forward(which, src, ref):
        for up in (0, 1):

            @pl.when(chain_goes(up, src))
            def _():
                chain_copy(which, up, src, ref).start()

    def plane_copy(which, src, j):
        packed, out = ((sx, rx), (sdy, rdy))[which]
        q = (p + j) % PLANE
        return remote(
            packed.at[src, q],
            out.at[src * PLANE + p],
            psend.at[which, src, j],
            precv.at[which, src, j],
            z * PLANE + q,
        )

    def own_copy(which, src):
        packed, out = ((sx, rx), (sdy, rdy))[which]
        return pltpu.make_async_copy(
            packed.at[src, p], out.at[src * PLANE + p], lsem.at[which, src]
        )

    def pack(which, src):
        ref, packed = ((gx, sx), (gdy, sdy))[which]
        codes = gm[src, 0:PLANE, :]
        weights = gm[src, PLANE : 2 * PLANE, :] if which else jnp.ones_like(codes)
        rows = one_hot_rows(codes, weights, cap)

        @pl.loop(0, width // tile)
        def _(c):
            cols = pl.ds(pl.multiple_of(c * tile, tile), tile)
            got = jnp.dot(rows, ref[src, :, cols], preferred_element_type=F32)
            for q in range(PLANE):
                packed[src, q, :, cols] = got[q * cap : (q + 1) * cap].astype(BF16)

        for j in range(1, PLANE):
            plane_copy(which, src, j).start()
        own_copy(which, src).start()

    def arrived(which, src):
        for j in range(1, PLANE):
            plane_copy(which, src, j).wait_recv()
        own_copy(which, src).wait()

    def row_copy(which, src):
        got, out = ((rx, ox), (rdy, ody))[which]
        blocks = pl.ds(src * PLANE, PLANE)
        return pltpu.make_async_copy(got.at[blocks], out.at[blocks], osem.at[which, src])

    def stage_copies(src):
        rows = pl.ds(pl.multiple_of(src * block, block), block)
        pairs = ((st_hid, hid_out), (st_dg, dg_out), (st_du, du_out), (st_sc, sc_out))
        return [
            pltpu.make_async_copy(held, out.at[rows], dsem.at[k])
            for k, (held, out) in enumerate(pairs)
        ]

    def compute(src, opening):
        arrived(0, src)
        row_copy(0, src).start()
        if opening:
            for k in range(3):
                weight_copy(k).wait()
        acc_g[...] = jnp.zeros_like(acc_g)
        acc_u[...] = jnp.zeros_like(acc_u)
        acc_h[...] = jnp.zeros_like(acc_h)

        @pl.loop(0, width // tile)
        def _(c):
            cols = pl.ds(pl.multiple_of(c * tile, tile), tile)
            rows = gather_rows(rx, src, cols)
            acc_g[...] += jnp.dot(rows, wg[cols, :], preferred_element_type=F32)
            acc_u[...] += jnp.dot(rows, wu[cols, :], preferred_element_type=F32)

        arrived(1, src)
        row_copy(1, src).start()

        @pl.loop(0, width // tile)
        def _(c):
            cols = pl.ds(pl.multiple_of(c * tile, tile), tile)
            acc_h[...] += contract(gather_rows(rdy, src, cols), wd[:, cols], 1, 1)

        if not opening:
            for copy in stage_copies(src):
                copy.wait()
        share = acc_g.shape[1]
        part = share // 4

        def slice_step(c, score):
            cols = pl.ds(pl.multiple_of(c * part, part), part)
            act, slope = silu_parts(acc_g[:, cols])
            up = acc_u[:, cols]
            d_hidden = acc_h[:, cols]
            hidden = (act * up).astype(BF16)
            st_hid[:, cols] = hidden
            st_dg[:, cols] = (d_hidden * up * slope).astype(BF16)
            st_du[:, cols] = (d_hidden * act).astype(BF16)
            return score + jnp.sum(hidden.astype(F32) * d_hidden, axis=1, keepdims=True)

        score = lax.fori_loop(0, 4, slice_step, jnp.zeros((block, 1), F32))
        lane = lax.broadcasted_iota(jnp.int32, (block, LANES), 1)
        st_sc[...] = jnp.where(lane == me, score, 0.0).astype(BF16)
        for copy in stage_copies(src):
            copy.start()

    forward(0, z, x_ref)
    forward(1, z, dy_ref)
    if fused:
        for k in range(3):
            weight_copy(k).start()
    gm[z] = meta_ref[z]
    for which in (0, 1):
        in_copy(which).wait()
        pack(which, z)

    def valid(src, dist):
        return (src >= 0) & (src < planes)

    def exchange_step(dist):
        for which in (0, 1):
            held = (gx, gdy)[which]
            for src in (z - dist, z + dist):

                @pl.when(valid(src, dist))
                def _():
                    remote(
                        held.at[src], held.at[src], zsend.at[which, 0, src],
                        zrecv.at[which, src], me
                    ).wait_recv()
                    forward(which, src, held.at[src])

        for src in (z - dist, z + dist):

            @pl.when(valid(src, dist))
            def _():
                remote(gm.at[src], gm.at[src], msend.at[0], mrecv.at[src], me).wait_recv()
                pack(0, src)
                pack(1, src)

    def compute_step(dist):
        for src in (z - dist, z + dist):

            @pl.when(valid(src, dist))
            def _():
                compute(src, False)

    exchange_step(1)
    if fused:
        compute(z, True)

    @pl.loop(2, planes)
    def _(dist):
        exchange_step(dist)
        if fused:
            compute_step(dist - 1)

    if fused:
        compute_step(planes - 1)
        for copy in stage_copies(z):
            copy.wait()

    gm_out[...] = gm[...]
    for k in range(1, planes):
        meta_copy(k).wait_send()

    @pl.loop(0, planes)
    def _(src):
        for which in (0, 1):
            for up in (0, 1):

                @pl.when(chain_goes(up, src))
                def _():
                    held = (gx, gdy)[which]
                    chain_copy(which, up, src, held.at[src]).wait_send()

            for j in range(1, PLANE):
                plane_copy(which, src, j).wait_send()
            if fused:
                row_copy(which, src).wait()
            else:
                arrived(which, src)


def dispatch(meta, tokens, cotangent, slots, cap, weights):
    planes = slots // PLANE
    tok, width = tokens.shape
    fused = weights is not None
    vmem = pl.BlockSpec(memory_space=pltpu.VMEM)
    anywhere = pl.BlockSpec(memory_space=pl.ANY)
    rows = jax.ShapeDtypeStruct((slots, cap, width), BF16)
    dma = pltpu.SemaphoreType.DMA
    out_shape = [rows, rows, jax.ShapeDtypeStruct((planes, 2 * PLANE, tok), F32)]
    out_specs = [anywhere, anywhere, vmem]
    scratch = [
        pltpu.VMEM((planes, 2 * PLANE, tok), F32),
        pltpu.VMEM((planes, tok, width), BF16),
        pltpu.VMEM((planes, tok, width), BF16),
        pltpu.VMEM((planes, PLANE, cap, width), BF16),
        pltpu.VMEM((planes, PLANE, cap, width), BF16),
    ]
    sems = [
        dma((planes,)),
        dma((planes,)),
        dma((2, 2, planes)),
        dma((2, planes)),
        dma((2, planes, PLANE)),
        dma((2, planes, PLANE)),
        dma((2, planes)),
    ]
    args = [meta, tokens, cotangent]
    if fused:
        share = weights[0].shape[1]
        block = PLANE * cap
        for columns in (share, share, share, LANES):
            out_shape.append(jax.ShapeDtypeStruct((slots * cap, columns), BF16))
            out_specs.append(anywhere)
        scratch += [pltpu.VMEM((slots, cap, width), BF16)] * 2
        scratch += [pltpu.VMEM(w.shape, BF16) for w in weights]
        scratch += [pltpu.VMEM((block, share), F32)] * 3
        scratch += [pltpu.VMEM((block, share), BF16)] * 3 + [pltpu.VMEM((block, LANES), BF16)]
        sems += [dma((3,)), dma((2, planes)), dma((4,))]
        args += list(weights)
    sems += [dma((2,))]
    return pl.pallas_call(
        functools.partial(dispatch_kernel, planes, fused),
        out_shape=out_shape,
        in_specs=[vmem] + [anywhere] * (len(args) - 1),
        out_specs=out_specs,
        scratch_shapes=scratch + sems,
        compiler_params=pltpu.CompilerParams(
            collective_id=0, has_side_effects=True, vmem_limit_bytes=VMEM_BYTES
        ),
    )(*args)


def combine_kernel(planes, fused, *refs):
    if fused:
        dg_ref, du_ref, sc_ref, wg_hbm, wu_hbm, gm_ref, dx_ref, found_ref = refs[:8]
        piece, wg, wu, rp, sp, rs, psend, precv, lsem, zsend, zrecv, wsem = refs[8:]
    else:
        piece, gm_ref, dx_ref, found_ref = refs[:4]
        rp, sp, rs, psend, precv, lsem, zsend, zrecv = refs[4:]
    me = lax.axis_index("expert")
    z, p = me // PLANE, me % PLANE
    cap, wide = piece.shape[1], piece.shape[2]
    width = wide - LANES
    tile = column_tile(width)
    block = PLANE * cap

    def weight_copy(k, c):
        rows = pl.ds(pl.multiple_of(c * tile, tile), tile)
        return pltpu.make_async_copy(
            (wg_hbm, wu_hbm)[k].at[rows], (wg, wu)[k].at[rows], wsem.at[k, c]
        )

    if fused:
        for c in range(width // tile):
            weight_copy(0, c).start()
            weight_copy(1, c).start()
    greet(planes, z, p)

    low = jnp.where(z < planes // 2, z, planes - 1 - z)

    def dest(i):
        if i == planes - 1:
            return z
        b = jnp.where(i < planes - 1 - low, planes - 1 - i, i - (planes - 1 - low))
        return jnp.where(z < planes // 2, b, planes - 1 - b)

    def plane_copy(b, j):
        q = (p + j) % PLANE
        return remote(
            piece.at[b * PLANE + q], rp.at[b, p], psend.at[b, j], precv.at[b, j], z * PLANE + q
        )

    def own_copy(b):
        return pltpu.make_async_copy(piece.at[b * PLANE + p], rp.at[b, p], lsem.at[b])

    def chain_copy(b, up):
        there = z + 1 if up else z - 1
        slot = b if up else jnp.where(b == there, planes, b)
        return remote(sp.at[b], rs.at[slot], zsend.at[b], zrecv.at[slot], there * PLANE + p)

    def make_piece(b, opening):
        if not fused:
            return
        rows = pl.ds(pl.multiple_of(b * block, block), block)

        @pl.loop(0, width // tile)
        def _(c):
            if opening:
                weight_copy(0, c).wait()
                weight_copy(1, c).wait()
            cols = pl.ds(pl.multiple_of(c * tile, tile), tile)
            got = contract(dg_ref[rows, :], wg[cols, :], 1, 1)
            got = got + contract(du_ref[rows, :], wu[cols, :], 1, 1)
            for q in range(PLANE):
                piece[b * PLANE + q, :, cols] = got[q * cap : (q + 1) * cap].astype(BF16)

        score = sc_ref[rows, :].astype(F32)
        for q in range(PLANE):
            piece[b * PLANE + q, :, width:wide] = score[q * cap : (q + 1) * cap].astype(BF16)

    def send_piece(b):
        for j in range(1, PLANE):
            plane_copy(b, j).start()
        own_copy(b).start()

    def partial(b, rows, cols):
        parts = [rp[b, q, :, cols].astype(F32) for q in range(PLANE)]
        return contract(rows, jnp.concatenate(parts, axis=0).astype(BF16), 0, 0)

    def arrived(b):
        for j in range(1, PLANE):
            plane_copy(b, j).wait_recv()
        own_copy(b).wait()
        codes = gm_ref[b, 0:PLANE, :]
        return one_hot_rows(codes, jnp.ones_like(codes), cap)

    def wait_sum(slot):
        remote(rs.at[slot], rs.at[slot], zsend.at[0], zrecv.at[slot], me).wait_recv()

    def each(body):
        @pl.loop(0, width // tile)
        def _(c):
            body(pl.ds(pl.multiple_of(c * tile, tile), tile))

        body(slice(width, wide))

    make_piece(dest(0), True)
    send_piece(dest(0))
    for i in range(planes - 1):
        b = dest(i)
        make_piece(dest(i + 1), False)
        rows = arrived(b)
        send_piece(dest(i + 1))
        begins = ((b > z) & (z == 0)) | ((b < z) & (z == planes - 1))

        @pl.when(begins)
        def _():
            def start(cols):
                sp[b, :, cols] = partial(b, rows, cols).astype(BF16)

            each(start)

        @pl.when(jnp.logical_not(begins))
        def _():
            wait_sum(b)

            def add(cols):
                sp[b, :, cols] = (partial(b, rows, cols) + rs[b, :, cols].astype(F32)).astype(BF16)

            each(add)

        @pl.when(b > z)
        def _():
            chain_copy(b, 1).start()

        @pl.when(b < z)
        def _():
            chain_copy(b, 0).start()

    own_rows = arrived(z)

    @pl.when(z > 0)
    def _():
        wait_sum(z)

    @pl.when(z < planes - 1)
    def _():
        wait_sum(planes)

    @pl.when(z == 0)
    def _():
        rs[0] = jnp.zeros_like(rs[0])

    @pl.when(z == planes - 1)
    def _():
        rs[planes] = jnp.zeros_like(rs[planes])

    def total(cols):
        acc = partial(z, own_rows, cols) + rs[z, :, cols].astype(F32)
        return acc + rs[planes, :, cols].astype(F32)

    @pl.loop(0, width // tile)
    def _(c):
        cols = pl.ds(pl.multiple_of(c * tile, tile), tile)
        dx_ref[:, cols] = total(cols).astype(BF16)

    found_ref[...] = total(slice(width, wide))

    @pl.loop(0, planes)
    def _(b):
        for j in range(1, PLANE):
            plane_copy(b, j).wait_send()

        @pl.when(b > z)
        def _():
            chain_copy(b, 1).wait_send()

        @pl.when(b < z)
        def _():
            chain_copy(b, 0).wait_send()


def combine(parts, gm, slots, cap, tok, width):
    planes = slots // PLANE
    wide = width + LANES
    fused = len(parts) > 1
    vmem = pl.BlockSpec(memory_space=pltpu.VMEM)
    anywhere = pl.BlockSpec(memory_space=pl.ANY)
    dma = pltpu.SemaphoreType.DMA
    scratch = [
        pltpu.VMEM((planes, PLANE, cap, wide), BF16),
        pltpu.VMEM((planes, tok, wide), BF16),
        pltpu.VMEM((planes + 1, tok, wide), BF16),
    ]
    sems = [
        dma((planes, PLANE)),
        dma((planes, PLANE)),
        dma((planes,)),
        dma((planes,)),
        dma((planes + 1,)),
    ]
    in_specs = [anywhere, vmem]
    if fused:
        scratch = [
            pltpu.VMEM((slots, cap, wide), BF16),
            pltpu.VMEM(parts[3].shape, BF16),
            pltpu.VMEM(parts[4].shape, BF16),
        ] + scratch
        sems += [dma((2, width // column_tile(width)))]
        in_specs = [vmem] * 3 + [anywhere] * 2 + [vmem]
    return pl.pallas_call(
        functools.partial(combine_kernel, planes, fused),
        out_shape=(
            jax.ShapeDtypeStruct((tok, width), BF16),
            jax.ShapeDtypeStruct((tok, LANES), F32),
        ),
        in_specs=in_specs,
        out_specs=(vmem, vmem),
        scratch_shapes=scratch + sems,
        compiler_params=pltpu.CompilerParams(
            collective_id=1, has_side_effects=True, vmem_limit_bytes=VMEM_BYTES
        ),
    )(*parts, gm)


def shards(tokens, cotangent, expert_ids, gate_probs, slot_expert, w_gate, w_up, w_down):
    slots = lax.axis_size("expert")
    here = lax.axis_index("expert")
    planes = slots // PLANE
    tok_rows, quarter = tokens.shape
    top = expert_ids.shape[1]
    experts = slots - max(2, slots // 8)
    capacity = max(2, 5 * tok_rows * top // (4 * experts))
    capacity = (capacity + 7) // 8 * 8
    width = w_gate.shape[1]
    total = slots * capacity
    hit = expert_ids[:, :, None] == slot_expert[None, None, :]
    probs = gate_probs.astype(F32)
    hits = hit.astype(F32)
    taken = jnp.sum(hits, axis=1)
    weight = jnp.sum(hits * probs[:, :, None], axis=1)
    row = jnp.arange(tok_rows, dtype=jnp.int32)
    earlier = (row[:, None] > row[None, :]).astype(BF16)
    rank = jnp.dot(earlier, taken.astype(BF16), preferred_element_type=F32)
    code = jnp.where(taken > 0.0, rank, -1.0)
    meta = jnp.concatenate(
        [code.T.reshape(planes, PLANE, tok_rows), weight.T.reshape(planes, PLANE, tok_rows)],
        axis=1,
    )
    wg = w_gate[0]
    wu = w_up[0]
    wd = w_down[0]
    slot = jnp.arange(slots, dtype=jnp.int32)
    repeat = (slot_expert[:, None] == slot_expert[None, :]) & (slot[:, None] > slot[None, :])
    first = jnp.logical_not(jnp.any(repeat, axis=1))
    plane_first = lax.dynamic_slice_in_dim(first, here // PLANE * PLANE, PLANE, 0)
    fused = lax.axis_size("dp") == 1
    if fused:
        part_x, part_dy, got_meta, hidden, d_gate_pre, d_up_pre, placed_scores = dispatch(
            meta, tokens, cotangent, slots, capacity, (wg, wu, wd)
        )
        xs = part_x.reshape(total, width)
        d_out = part_dy.reshape(total, width)
        parts = (d_gate_pre, d_up_pre, placed_scores, wg, wu)
    else:
        part_x, part_dy, got_meta = dispatch(meta, tokens, cotangent, slots, capacity, None)
        xs = lax.all_gather(part_x, "dp", axis=2, tiled=True).reshape(total, width)
        d_out = lax.all_gather(part_dy, "dp", axis=2, tiled=True).reshape(total, width)
        gate = contract(xs, wg, 1, 0)
        up = contract(xs, wu, 1, 0)
        d_hidden = contract(d_out, wd, 1, 1)
        act, slope = silu_parts(gate)
        hidden = (act * up).astype(BF16)
        score = jnp.sum(hidden.astype(F32) * d_hidden, axis=1)
        d_gate_pre = (d_hidden * up * slope).astype(BF16)
        d_up_pre = (d_hidden * act).astype(BF16)
        piece = contract(d_gate_pre, wg, 1, 1) + contract(d_up_pre, wu, 1, 1)
        summed = lax.psum_scatter(
            piece.astype(BF16).reshape(slots, capacity, width),
            "dp",
            scatter_dimension=2,
            tiled=True,
        )
        scores = lax.psum(score.reshape(slots, capacity), "dp").astype(BF16)
        lane = jnp.arange(LANES, dtype=jnp.int32)
        placed_scores = jnp.where(lane == here, scores[:, :, None], 0.0).astype(BF16)
        parts = (jnp.concatenate([summed, placed_scores], axis=2),)
    back_code = jnp.where(plane_first[None, :, None], got_meta[:, :PLANE], -1.0)
    d_tokens, found = combine(parts, back_code, slots, capacity, tok_rows, quarter)
    grad_down = contract(hidden, d_out, 0, 0).astype(BF16)[None]
    grad_gate = contract(xs, d_gate_pre, 0, 0).astype(BF16)[None]
    grad_up = contract(xs, d_up_pre, 0, 0).astype(BF16)[None]
    listed = jnp.where(hit & first[None, None, :], found[:, None, :slots], 0.0)
    d_probs = jnp.sum(listed, axis=2) / probs
    return (d_tokens, d_probs, grad_gate, grad_up, grad_down)


def solution(mesh):
    placed = (
        P("expert", "dp"),
        P("expert", "dp"),
        P("expert", None),
        P("expert", None),
        P(),
        P("expert", None, "dp"),
        P("expert", None, "dp"),
        P("expert", "dp", None),
    )
    return jax.shard_map(
        shards,
        mesh=mesh,
        in_specs=placed,
        out_specs=(
            P("expert", "dp"),
            P("expert", None),
            P("expert", None, "dp"),
            P("expert", None, "dp"),
            P("expert", "dp", None),
        ),
        check_vma=False,
    )
```

time: 341 us -> 302 us (0.89); the launches traced: 341 us -> 297 us
  matrix products: 73.7 us -> 27.1 us
  Pallas kernels: 253 us -> 262 us
  other arithmetic: 10.7 us -> 5.09 us
    dot_general x8 -> x3, matrix products: 73.6 us -> 27 us  [contract(): lax.dot_general(left, right, (((left_dim,), (right_dim,)), ((), ())), pre...]
    pallas_call x2, Pallas kernels: 253 us -> 262 us  [the longest x1 163 us: dispatch(): pl.pallas_call(functools.partial(dispatch_kernel, planes, fused), out_sha...]
    concatenate x1 -> x0, other arithmetic: 5.46 us -> none  [shards(): jnp.concatenate([summed, placed_scores], axis=2)]
where the time goes in v2:
time: 302 us; the launch traced here: 297 us
  Pallas kernels  262 us (87%)
  matrix products  27.1 us (9%)
  other arithmetic  5.09 us (2%)
    pallas_call x1, Pallas kernels, dispatch(): pl.pallas_call(functools.partial(dispatch_kernel, planes, fused), out_sha...  163 us
    pallas_call x1, Pallas kernels, combine(): pl.pallas_call(functools.partial(combine_kernel, planes, fused), out_shap...  98.3 us
    dot_general x3, matrix products, contract(): lax.dot_general(left, right, (((left_dim,), (right_dim,)), ((), ())), pre...  27 us

profile of v2, /device:TPU:0, one launch (start us, length us, event | category | flops | bytes accessed | tf_op | source)
XLA Modules:
  0.0 296.5 jit_solution(8271693019716117352)
XLA Ops:
  0.6 0.9 fusion.7
  1.6 0.1 dynamic_slice.3
  1.7 0.7 convert_element_type.21
  2.3 0.8 fusion.4
  3.1 0.1 fusion.3
  3.2 0.6 pad_maximum_fusion.refs_0_
  3.9 163.4 %shard_map.119 = (bf16[32,24,3584]{2,1,0:T(8,128)(2,1)}, bf16[32,24,3584]{2,1,0:T(8,128)(2,1)}, f32[4,16,128]{2,1,0:T(8,128)}, bf16[768,1024]{1,0:T(8,128)(2,1)}...) custom-call(f32[4,16,128]{2,1,0:T(8,128)} %pad_maximum_fusion.refs_0_, ...), custom_call_target="tpu_custom_call" | custom-call | tf_op jit(solution)/shard_map/pallas_call | solution.py:350
  167.3 1.4 slice_select_fusion.refs_5_
  168.7 0.0 copy-start.3
  168.7 0.0 copy-start.5
  168.7 0.0 copy-start.4
  168.7 0.0 copy-start.1
  168.7 98.3 %shard_map.120 = (bf16[128,3584]{1,0:T(8,128)(2,1)}, f32[128,128]{1,0:T(8,128)}) custom-call(bf16[768,1024]{1,0:T(8,128)(2,1)} %get-tuple-element.14.refs_0_, bf16[768,1024]{1,0:T(8,128)(2,1)} %get-tuple-element.15.refs_1_, bf16[768,128]{1,0:T(8,128)(2,1)} %get-tuple-element.16.refs_2_, bf16[3584,1024]{1,0:T(8,128)(2,1)} %bitcast.26, ...), custom_call_target="tpu_custom_call" | custom-call | tf_op jit(solution)/shard_map/pallas_call | solution.py:560
  267.0 0.9 copy.15
  267.9 0.0 copy-done.3
  267.9 0.0 copy-done.5
  267.9 0.1 select_reduce_fusion
  268.0 0.0 copy-done.4
  268.0 0.6 convert_divide_fusion
  268.6 0.0 copy-done.1
  268.6 0.0 copy-start
  268.6 0.0 copy-start.7
  268.6 10.7 %fusion.1 = bf16[1,3584,1024]{2,1,0:T(8,128)(2,1)} fusion(bf16[768,3584]{1,0:T(8,128)(2,1)} %bitcast.33, bf16[768,1024]{1,0:T(8,128)(2,1)S(1)} %copy-done.1), kind=kOutput, calls=%fused_computation.4 | convolution fusion | flops 5640814592 | bytes 14417920 | tf_op jit(solution)/shard_map/dot_general | solution.py:23
  279.3 0.0 copy-done
  279.3 0.0 copy-done.7
  279.3 0.0 copy-start.6
  279.3 0.0 copy-start.8
  279.3 8.1 %fusion = bf16[1,3584,1024]{2,1,0:T(8,128)(2,1)} fusion(bf16[768,3584]{1,0:T(8,128)(2,1)S(1)} %bitcast.34, bf16[768,1024]{1,0:T(8,128)(2,1)S(1)} %copy-done), kind=kOutput, calls=%fused_computation.3 | convolution fusion | flops 5640814592 | bytes 14417920 | tf_op jit(solution)/shard_map/dot_general | solution.py:23
  287.4 0.0 copy-done.6
  287.4 0.0 copy-done.8
  287.4 0.0 copy-start.2
  287.4 8.2 %fusion.2 = bf16[1,1024,3584]{2,1,0:T(8,128)(2,1)} fusion(bf16[768,1024]{1,0:T(8,128)(2,1)S(1)} %copy-done.8, bf16[768,3584]{1,0:T(8,128)(2,1)S(1)} %bitcast.32), kind=kOutput, calls=%fused_computation.5 | convolution fusion | flops 5640814592 | bytes 14417920 | tf_op jit(solution)/shard_map/dot_general | solution.py:23
  295.6 0.0 copy-done.2
  295.6 0.9 copy.17
  (1 shorter events, 0.0 us)
Async XLA Ops:
  168.7 99.2 %copy-start.3 = (s32[128,4]{0,1:T(4,128)S(1)}, s32[128,4]{0,1:T(4,128)}, u32[]{:S(2)}) copy-start(s32[128,4]{0,1:T(4,128)} %param.10) | copy-start | bytes 6148
  168.7 99.2 %copy-start.5 = (s32[32]{0:T(128)S(1)}, s32[32]{0:T(128)}, u32[]{:S(2)}) copy-start(s32[32]{0:T(128)} %param.12) | copy-start | bytes 388
  168.7 99.3 %copy-start.4 = (bf16[128,4]{0,1:T(4,128)(2,1)S(1)}, bf16[128,4]{0,1:T(4,128)(2,1)}, u32[]{:S(2)}) copy-start(bf16[128,4]{0,1:T(4,128)(2,1)} %param.11) | copy-start | bytes 3076
  168.7 99.9 %copy-start.1 = (bf16[768,1024]{1,0:T(8,128)(2,1)S(1)}, bf16[768,1024]{1,0:T(8,128)(2,1)}, u32[]{:S(2)}) copy-start(bf16[768,1024]{1,0:T(8,128)(2,1)} %get-tuple-element.15.refs_1_) | copy-start | bytes 4718596
  268.6 10.7 %copy-start = (bf16[768,1024]{1,0:T(8,128)(2,1)S(1)}, bf16[768,1024]{1,0:T(8,128)(2,1)}, u32[]{:S(2)}) copy-start(bf16[768,1024]{1,0:T(8,128)(2,1)} %get-tuple-element.14.refs_0_) | copy-start | bytes 4718596
  268.6 10.7 %copy-start.7 = (bf16[32,24,3584]{2,1,0:T(8,128)(2,1)S(1)}, bf16[32,24,3584]{2,1,0:T(8,128)(2,1)}, u32[]{:S(2)}) copy-start(bf16[32,24,3584]{2,1,0:T(8,128)(2,1)} %get-tuple-element.20) | copy-start | bytes 16515076
  279.3 8.1 %copy-start.6 = (bf16[32,24,3584]{2,1,0:T(8,128)(2,1)S(1)}, bf16[32,24,3584]{2,1,0:T(8,128)(2,1)}, u32[]{:S(2)}) copy-start(bf16[32,24,3584]{2,1,0:T(8,128)(2,1)} %get-tuple-element.22) | copy-start | bytes 16515076
  279.3 8.1 %copy-start.8 = (bf16[768,1024]{1,0:T(8,128)(2,1)S(1)}, bf16[768,1024]{1,0:T(8,128)(2,1)}, u32[]{:S(2)}) copy-start(bf16[768,1024]{1,0:T(8,128)(2,1)} %get-tuple-element.21) | copy-start | bytes 4718596
  287.4 8.2 %copy-start.2 = (bf16[128,3584]{1,0:T(8,128)(2,1)S(1)}, bf16[128,3584]{1,0:T(8,128)(2,1)}, u32[]{:S(2)}) copy-start(bf16[128,3584]{1,0:T(8,128)(2,1)} %get-tuple-element.30) | copy-start | bytes 2752516

commit v3 on v2

--- a/solution.py
+++ b/solution.py
@@ -229,56 +229,81 @@
         for copy in stage_copies(src):
             copy.start()
 
+    def valid(src):
+        return (src >= 0) & (src < planes)
+
+    def take(which, dist):
+        held = (gx, gdy)[which]
+        for src in (z - dist, z + dist):
+
+            @pl.when(valid(src))
+            def _():
+                remote(
+                    held.at[src], held.at[src], zsend.at[which, 0, src], zrecv.at[which, src], me
+                ).wait_recv()
+                forward(which, src, held.at[src])
+
+    def pack_step(which, dist):
+        for src in (z - dist, z + dist):
+
+            @pl.when(valid(src))
+            def _():
+                if which == 0:
+                    remote(gm.at[src], gm.at[src], msend.at[0], mrecv.at[src], me).wait_recv()
+                pack(which, src)
+
+    def compute_step(dist):
+        for src in (z - dist, z + dist):
+
+            @pl.when(valid(src))
+            def _():
+                compute(src, False)
+
     forward(0, z, x_ref)
-    forward(1, z, dy_ref)
     if fused:
         for k in range(3):
             weight_copy(k).start()
     gm[z] = meta_ref[z]
-    for which in (0, 1):
-        in_copy(which).wait()
-        pack(which, z)
-
-    def valid(src, dist):
-        return (src >= 0) & (src < planes)
-
-    def exchange_step(dist):
-        for which in (0, 1):
-            held = (gx, gdy)[which]
-            for src in (z - dist, z + dist):
-
-                @pl.when(valid(src, dist))
-                def _():
-                    remote(
-                        held.at[src], held.at[src], zsend.at[which, 0, src],
-                        zrecv.at[which, src], me
-                    ).wait_recv()
-                    forward(which, src, held.at[src])
-
-        for src in (z - dist, z + dist):
-
-            @pl.when(valid(src, dist))
-            def _():
-                remote(gm.at[src], gm.at[src], msend.at[0], mrecv.at[src], me).wait_recv()
-                pack(0, src)
-                pack(1, src)
-
-    def compute_step(dist):
-        for src in (z - dist, z + dist):
-
-            @pl.when(valid(src, dist))
-            def _():
-                compute(src, False)
-
-    exchange_step(1)
-    if fused:
-        compute(z, True)
-
-    @pl.loop(2, planes)
-    def _(dist):
-        exchange_step(dist)
+    in_copy(0).wait()
+    in_copy(1).wait()
+    pack(0, z)
+    for up in (0, 1):
+
+        @pl.when(chain_goes(up, z))
+        def _():
+            chain_copy(0, up, z, x_ref).wait_send()
+
+    forward(1, z, dy_ref)
+    take(0, 1)
+    pack(1, z)
+    pack_step(0, 1)
+
+    def stage(dist, last):
+        take(1, dist)
+        if not last:
+            take(0, dist + 1)
+        pack_step(1, dist)
+        if not last:
+            pack_step(0, dist + 1)
+
+    if planes > 2:
+        stage(1, False)
         if fused:
-            compute_step(dist - 1)
+            compute(z, True)
+
+        @pl.loop(2, planes - 1)
+        def _(dist):
+            stage(dist, False)
+            if fused:
+                compute_step(dist - 1)
+
+        stage(planes - 1, True)
+        if fused:
+            compute_step(planes - 2)
+    else:
+        stage(1, True)
+        if fused:
+            compute(z, True)
 
     if fused:
         compute_step(planes - 1)
@@ -294,7 +319,9 @@
         for which in (0, 1):
             for up in (0, 1):
 
-                @pl.when(chain_goes(up, src))
+                unmet = chain_goes(up, src) & (src != z) if which == 0 else chain_goes(up, src)
+
+                @pl.when(unmet)
                 def _():
                     held = (gx, gdy)[which]
                     chain_copy(which, up, src, held.at[src]).wait_send()
@@ -572,6 +599,39 @@
     )(*parts, gm)
 
 
+def grads_kernel(xs, d_out, hidden, d_gate, d_up, g_gate, g_up, g_down, hidden_t):
+    @pl.when(pl.program_id(0) == 0)
+    def _():
+        hidden_t[...] = hidden[...].T
+
+    xs_t = xs[...].T
+    g_gate[...] = jnp.dot(xs_t, d_gate[...], preferred_element_type=F32).astype(BF16)
+    g_up[...] = jnp.dot(xs_t, d_up[...], preferred_element_type=F32).astype(BF16)
+    g_down[...] = jnp.dot(hidden_t[...], d_out[...], preferred_element_type=F32).astype(BF16)
+
+
+def weight_grads(xs, d_out, hidden, d_gate, d_up):
+    rows, width = xs.shape
+    share = hidden.shape[1]
+    tile = column_tile(width)
+    whole = pl.BlockSpec((rows, share), lambda i: (0, 0))
+    piece = pl.BlockSpec((rows, tile), lambda i: (0, i))
+    across = pl.BlockSpec((tile, share), lambda i: (i, 0))
+    return pl.pallas_call(
+        grads_kernel,
+        grid=(width // tile,),
+        out_shape=(
+            jax.ShapeDtypeStruct((width, share), BF16),
+            jax.ShapeDtypeStruct((width, share), BF16),
+            jax.ShapeDtypeStruct((share, width), BF16),
+        ),
+        in_specs=[piece, piece, whole, whole, whole],
+        out_specs=(across, across, pl.BlockSpec((share, tile), lambda i: (0, i))),
+        scratch_shapes=[pltpu.VMEM((share, rows), BF16)],
+        compiler_params=pltpu.CompilerParams(vmem_limit_bytes=VMEM_BYTES),
+    )(xs, d_out, hidden, d_gate, d_up)
+
+
 def shards(tokens, cotangent, expert_ids, gate_probs, slot_expert, w_gate, w_up, w_down):
     slots = lax.axis_size("expert")
     here = lax.axis_index("expert")
@@ -636,12 +696,10 @@
         parts = (jnp.concatenate([summed, placed_scores], axis=2),)
     back_code = jnp.where(plane_first[None, :, None], got_meta[:, :PLANE], -1.0)
     d_tokens, found = combine(parts, back_code, slots, capacity, tok_rows, quarter)
-    grad_down = contract(hidden, d_out, 0, 0).astype(BF16)[None]
-    grad_gate = contract(xs, d_gate_pre, 0, 0).astype(BF16)[None]
-    grad_up = contract(xs, d_up_pre, 0, 0).astype(BF16)[None]
+    grad_gate, grad_up, grad_down = weight_grads(xs, d_out, hidden, d_gate_pre, d_up_pre)
     listed = jnp.where(hit & first[None, None, :], found[:, None, :slots], 0.0)
     d_probs = jnp.sum(listed, axis=2) / probs
-    return (d_tokens, d_probs, grad_gate, grad_up, grad_down)
+    return (d_tokens, d_probs, grad_gate[None], grad_up[None], grad_down[None])
 
 
 def solution(mesh):

time: 302 us -> 293 us (0.970)
  matrix products: 27.1 us -> 0.14 us
  Pallas kernels: 262 us -> 279 us
    dot_general x3 -> x0, matrix products: 27 us -> none  [contract(): lax.dot_general(left, right, (((left_dim,), (right_dim,)), ((), ())), pre...]
    pallas_call x0 -> x1, Pallas kernels: none -> 23 us  [weight_grads(): pl.pallas_call(grads_kernel, grid=(width // tile,), out_shape=(jax.ShapeD...]
    pallas_call x1, Pallas kernels: 163 us -> 158 us  [dispatch(): pl.pallas_call(functools.partial(dispatch_kernel, planes, fused), out_sha...]
where the time goes in v3:
time: 293 us; the launch traced here: 287 us
  Pallas kernels  279 us (95%)
  other arithmetic  5.09 us (2%)
    pallas_call x1, Pallas kernels, dispatch(): pl.pallas_call(functools.partial(dispatch_kernel, planes, fused), out_sha...  158 us
    pallas_call x1, Pallas kernels, combine(): pl.pallas_call(functools.partial(combine_kernel, planes, fused), out_shap...  98.1 us
    pallas_call x1, Pallas kernels, weight_grads(): pl.pallas_call(grads_kernel, grid=(width // tile,), out_shape=(jax.ShapeD...  23 us

profile of v3, /device:TPU:0, one launch (start us, length us, event | category | flops | bytes accessed | tf_op | source)
XLA Modules:
  0.0 287.0 jit_solution(4805554226393457429)
XLA Ops:
  0.6 0.9 fusion.4
  1.6 0.1 dynamic_slice.3
  1.7 0.7 convert_element_type.12
  2.3 0.8 fusion.1
  3.1 0.1 fusion
  3.2 0.6 pad_maximum_fusion.refs_0_
  3.9 158.0 %shard_map.119 = (bf16[32,24,3584]{2,1,0:T(8,128)(2,1)}, bf16[32,24,3584]{2,1,0:T(8,128)(2,1)}, f32[4,16,128]{2,1,0:T(8,128)}, bf16[768,1024]{1,0:T(8,128)(2,1)}...) custom-call(f32[4,16,128]{2,1,0:T(8,128)} %pad_maximum_fusion.refs_0_, ...), custom_call_target="tpu_custom_call" | custom-call | tf_op jit(solution)/shard_map/pallas_call | solution.py:377
  161.9 1.4 slice_select_fusion.refs_5_
  163.3 0.0 copy-start.1
  163.3 0.0 copy-start.3
  163.3 0.0 copy-start.2
  163.3 98.1 %shard_map.120 = (bf16[128,3584]{1,0:T(8,128)(2,1)}, f32[128,128]{1,0:T(8,128)}) custom-call(bf16[768,1024]{1,0:T(8,128)(2,1)} %get-tuple-element.17.refs_0_.d_gate, bf16[768,1024]{1,0:T(8,128)(2,1)} %get-tuple-element.18.refs_1_.d_up, bf16[768,128]{1,0:T(8,128)(2,1)} %get-tuple-element.19.refs_2_, bf16[3584,1024]{1,0:T(8,128)(2,1)} %bitcast.17, ...), custom_call_target="tpu_custom_call" | custom-call | tf_op jit(solution)/shard_map/pallas_call | solution.py:587
  261.4 0.9 copy.15
  262.3 0.0 copy-done.1
  262.3 0.0 copy-done.3
  262.3 0.1 select_reduce_fusion
  262.4 0.0 copy-done.2
  262.4 0.6 convert_divide_fusion
  263.0 0.0 copy-start
  263.0 23.0 %shard_map.121 = (bf16[3584,1024]{1,0:T(8,128)(2,1)}, bf16[3584,1024]{1,0:T(8,128)(2,1)}, bf16[1024,3584]{1,0:T(8,128)(2,1)}) custom-call(bf16[768,3584]{1,0:T(8,128)(2,1)} %bitcast.21, bf16[768,3584]{1,0:T(8,128)(2,1)} %bitcast.22, bf16[768,1024]{1,0:T(8,128)(2,1)} %get-tuple-element.25.hidden, bf16[768,1024]{1,0:T(8,128)(2,1)} %get-tuple-element.17.refs_0_.d_gate, ...), custom_call_target="tpu_custom_call" | custom-call | tf_op jit(solution)/shard_map/pallas_call | solution.py:620
  286.1 0.0 copy-done
  286.1 0.9 copy.17
  (1 shorter events, 0.0 us)
Async XLA Ops:
  163.3 99.0 %copy-start.1 = (s32[128,4]{0,1:T(4,128)S(1)}, s32[128,4]{0,1:T(4,128)}, u32[]{:S(2)}) copy-start(s32[128,4]{0,1:T(4,128)} %param.10) | copy-start | bytes 6148
  163.3 99.0 %copy-start.3 = (s32[32]{0:T(128)S(1)}, s32[32]{0:T(128)}, u32[]{:S(2)}) copy-start(s32[32]{0:T(128)} %param.12) | copy-start | bytes 388
  163.3 99.1 %copy-start.2 = (bf16[128,4]{0,1:T(4,128)(2,1)S(1)}, bf16[128,4]{0,1:T(4,128)(2,1)}, u32[]{:S(2)}) copy-start(bf16[128,4]{0,1:T(4,128)(2,1)} %param.11) | copy-start | bytes 3076
  263.0 23.1 %copy-start = (bf16[128,3584]{1,0:T(8,128)(2,1)S(1)}, bf16[128,3584]{1,0:T(8,128)(2,1)}, u32[]{:S(2)}) copy-start(bf16[128,3584]{1,0:T(8,128)(2,1)} %get-tuple-element.36) | copy-start | bytes 2752516
